TPU v7x, 32 devices: a whole 2x2x4 slice. The times are simulated.
32 devices in a mesh: wide: 8 (over z, x), narrow: 4 (over y, core).
Axes of the slice: x: 2, y: 2, z: 4, core: 2. Of those that a mesh axis runs over, the one named last changes fastest.
Arguments:
- tokens: bfloat16 [12288, 768], P(('wide', 'narrow')), may hold values from -6 to 6
- type_ids: int32 [12288], P(('wide', 'narrow')), may hold values from 0 to 1
- segment_ids: int32 [24, 512], P('wide'), may hold values from 0 to 2, as said below
- cotangent: bfloat16 [12288, 768], P(('wide', 'narrow')), may hold values from -6 to 6
- type_table: float32 [2, 768], replicated, may hold values from -3 to 3
- type_first: float32 [2, 768], replicated, may hold values from -448 to 448
- type_second: float32 [2, 768], replicated, may hold values from 6144 to 24576
- norm_gains: float32 [2, 768], replicated, may hold values from 0.5 to 1.5
- gains_first: float32 [2, 768], replicated, may hold values from -640 to 640
- gains_second: float32 [2, 768], replicated, may hold values from 12288 to 49152
- biases: float32 [6, 768], replicated, may hold values from -1.25 to 1.25
- biases_first: float32 [6, 768], replicated, may hold values from -640 to 640
- biases_second: float32 [6, 768], replicated, may hold values from 12288 to 49152
- qkv_weight: float32 [3, 768, 768], P(None, 'wide', 'narrow'), may hold values from -0.21875 to 0.21875
- qkv_first: float32 [3, 768, 768], P(None, 'wide', 'narrow'), may hold values from -640 to 640
- qkv_second: float32 [3, 768, 768], P(None, 'wide', 'narrow'), may hold values from 12288 to 49152
- out_weight: float32 [768, 768], P('narrow', 'wide'), may hold values from -0.875 to 0.875
- out_first: float32 [768, 768], P('narrow', 'wide'), may hold values from -192 to 192
- out_second: float32 [768, 768], P('narrow', 'wide'), may hold values from 1105.92 to 4423.68
- up_weight: float32 [768, 3072], P(None, ('wide', 'narrow')), may hold values from -0.21875 to 0.21875
- up_first: float32 [768, 3072], P(None, ('wide', 'narrow')), may hold values from -224 to 224
- up_second: float32 [768, 3072], P(None, ('wide', 'narrow')), may hold values from 1474.56 to 6144
- up_bias: float32 [3072], P(('wide', 'narrow')), may hold values from -1.25 to 1.25
- up_bias_first: float32 [3072], P(('wide', 'narrow')), may hold values from -224 to 224
- up_bias_second: float32 [3072], P(('wide', 'narrow')), may hold values from 1474.56 to 6144
- down_weight: float32 [3072, 768], P(('wide', 'narrow')), may hold values from -0.109375 to 0.109375
- down_first: float32 [3072, 768], P(('wide', 'narrow')), may hold values from -448 to 448
- down_second: float32 [3072, 768], P(('wide', 'narrow')), may hold values from 4915.2 to 19660.8
Outputs:
- activations: bfloat16 [12288, 768], P(('wide', 'narrow'))
- input_grad: float32 [12288, 768], P(('wide', 'narrow'))
- type_new: float32 [2, 768], replicated
- type_first_new: float32 [2, 768], replicated
- type_second_new: float32 [2, 768], replicated
- gains_new: float32 [2, 768], replicated
- gains_first_new: float32 [2, 768], replicated
- gains_second_new: float32 [2, 768], replicated
- biases_new: float32 [6, 768], replicated
- biases_first_new: float32 [6, 768], replicated
- biases_second_new: float32 [6, 768], replicated
- qkv_new: float32 [3, 768, 768], P(None, 'wide', 'narrow')
- qkv_first_new: float32 [3, 768, 768], P(None, 'wide', 'narrow')
- qkv_second_new: float32 [3, 768, 768], P(None, 'wide', 'narrow')
- out_new: float32 [768, 768], P('narrow', 'wide')
- out_first_new: float32 [768, 768], P('narrow', 'wide')
- out_second_new: float32 [768, 768], P('narrow', 'wide')
- up_new: float32 [768, 3072], P(None, ('wide', 'narrow'))
- up_first_new: float32 [768, 3072], P(None, ('wide', 'narrow'))
- up_second_new: float32 [768, 3072], P(None, ('wide', 'narrow'))
- up_bias_new: float32 [3072], P(('wide', 'narrow'))
- up_bias_first_new: float32 [3072], P(('wide', 'narrow'))
- up_bias_second_new: float32 [3072], P(('wide', 'narrow'))
- down_new: float32 [3072, 768], P(('wide', 'narrow'))
- down_first_new: float32 [3072, 768], P(('wide', 'narrow'))
- down_second_new: float32 [3072, 768], P(('wide', 'narrow'))
Inputs may be any that keep to these rules, and one draw needn't show every extreme that they name: `segment_ids`: each packed sequence holds exactly three documents, numbered 0, 1, 2 in order along its 512 rows, each of one row or more; the ids never fall.
All inputs are finite; a program needn't handle non-finite values.
Results may differ from a plain program's by a relative error of at most 0.012.
Values may be sent and summed in bfloat16 or wider, within the bound.
A program may use at most 192 MiB of HBM per device.

v0:
```python
import jax
import jax.numpy as jnp
from jax import lax
from jax.sharding import PartitionSpec as P

D = 768
HD = 64
FF = 3072
STEP = 5


norm_eps = 1e-06
masked_score = -1e30


def in_blocks(value, dim, size):
    shape = value.shape
    tiles = value.reshape(*shape[:dim], size, shape[dim] // size, *shape[dim + 1 :])
    return jnp.moveaxis(tiles, dim, 0)


def sent_and_summed(value, axis, dim):
    tiles = in_blocks(value, dim, lax.axis_size(axis))
    arrived = lax.all_to_all(tiles, axis, split_axis=0, concat_axis=0, tiled=True)
    return arrived.astype(jnp.float32).sum(axis=0)


def norm_rows(values, gain, shift):
    center = jnp.mean(values, axis=-1, keepdims=True)
    spread = values - center
    variance = jnp.mean(spread * spread, axis=-1, keepdims=True)
    return spread * lax.rsqrt(variance + norm_eps) * gain + shift


def gelu_exact(values):
    return jax.nn.gelu(values, approximate=False)


def times_transposed(left_mat, right_mat):
    return lax.dot_general(
        left_mat, right_mat, (((1,), (1,)), ((), ())), preferred_element_type=jnp.float32
    )


def transposed_times(left_mat, right_mat):
    return lax.dot_general(
        left_mat, right_mat, (((0,), (0,)), ((), ())), preferred_element_type=jnp.float32
    )


def adam_update(weight_in, moment_one, moment_two, gradient, step_rate):
    moment_one = 0.5 * moment_one + 0.5 * gradient
    moment_two = 0.5 * moment_two + 0.5 * gradient * gradient
    correction = 1.0 - 0.5**STEP
    direction = moment_one / correction / (jnp.sqrt(moment_two / correction) + 1e-08)
    return (weight_in - step_rate * (direction + 0.01 * weight_in), moment_one, moment_two)


def step_rates():
    return (0.5, 0.4, 0.4, D ** (-0.5), 4.0 * D ** (-0.5), D ** (-0.5), 0.4, FF ** (-0.5))


def group_rows(values):
    return lax.all_gather(values, "narrow", axis=0, tiled=True)


def group_sums(term_fn, local_rows):
    return lax.psum_scatter(
        term_fn(jnp.int32(0), lax.axis_size("narrow") * local_rows).astype(jnp.bfloat16),
        "narrow",
        scatter_dimension=0,
        tiled=True,
    ).astype(jnp.float32)


def masked_scores(queries, key_rows, segment):
    raw_scores = jnp.einsum(
        "qhd,khd->hqk", queries, key_rows, preferred_element_type=jnp.float32
    ) * HD ** (-0.5)
    same_doc = segment[:, None] == segment[None, :]
    return jnp.where(same_doc[None, :, :], raw_scores, masked_score)


def pack_forward(pack_item):
    queries, key_rows, values, segment = pack_item
    scores = masked_scores(queries, key_rows, segment)
    highest = jnp.max(scores, axis=-1, keepdims=True)
    exponentials = jnp.exp(scores - highest)
    totals = jnp.sum(exponentials, axis=-1, keepdims=True)
    weights = exponentials / totals
    attended = jnp.einsum(
        "hqk,khd->qhd", weights.astype(jnp.bfloat16), values, preferred_element_type=jnp.float32
    )
    return (attended.astype(jnp.bfloat16), (highest + jnp.log(totals))[:, :, 0])


def pack_backward(pack_item):
    queries, key_rows, values, segment, log_totals, grad_attended = pack_item
    scores = masked_scores(queries, key_rows, segment)
    weights = jnp.exp(scores - log_totals[:, :, None])
    grad_values = jnp.einsum(
        "hqk,qhd->khd",
        weights.astype(jnp.bfloat16),
        grad_attended,
        preferred_element_type=jnp.float32,
    )
    grad_weights = jnp.einsum(
        "qhd,khd->hqk", grad_attended, values, preferred_element_type=jnp.float32
    )
    center = jnp.sum(weights * grad_weights, axis=-1, keepdims=True)
    grad_scores = (weights * (grad_weights - center)).astype(jnp.bfloat16)
    grad_queries = jnp.einsum(
        "hqk,khd->qhd", grad_scores, key_rows, preferred_element_type=jnp.float32
    ) * HD ** (-0.5)
    grad_keys = jnp.einsum(
        "hqk,qhd->khd", grad_scores, queries, preferred_element_type=jnp.float32
    ) * HD ** (-0.5)
    return (
        grad_queries.astype(jnp.bfloat16),
        grad_keys.astype(jnp.bfloat16),
        grad_values.astype(jnp.bfloat16),
    )


def shards(
    tokens,
    type_ids,
    segment_ids,
    cotangent,
    type_table,
    type_first,
    type_second,
    norm_gains,
    gains_first,
    gains_second,
    biases,
    biases_first,
    biases_second,
    qkv_weight,
    qkv_first,
    qkv_second,
    out_weight,
    out_first,
    out_second,
    up_weight,
    up_first,
    up_second,
    up_bias,
    up_bias_first,
    up_bias_second,
    down_weight,
    down_first,
    down_second,
):
    local_rows = tokens.shape[0]
    model_width = tokens.shape[1]
    head_cols = qkv_weight.shape[2]
    heads_here = head_cols // HD
    pack_count = segment_ids.shape[0]
    pack_rows = segment_ids.shape[1]
    group_count = pack_count * pack_rows
    narrow_index = lax.axis_index("narrow")
    qkv_low = qkv_weight.astype(jnp.bfloat16)
    out_low = out_weight.astype(jnp.bfloat16)
    up_low = up_weight.astype(jnp.bfloat16)
    up_bias_low = up_bias.astype(jnp.bfloat16)
    down_low = down_weight.astype(jnp.bfloat16)
    qkv_full, out_rows = (
        lax.all_gather(qkv_low, "wide", axis=1, tiled=True),
        lax.all_gather(out_low, "wide", axis=1, tiled=True),
    )
    up_cols, up_bias_cols, down_rows = (
        lax.all_gather(up_low, ("wide", "narrow"), axis=1, tiled=True),
        lax.all_gather(up_bias_low, ("wide", "narrow"), axis=0, tiled=True),
        lax.all_gather(down_low, ("wide", "narrow"), axis=0, tiled=True),
    )
    is_image = (type_ids == 1)[:, None]
    embedded = tokens.astype(jnp.float32) + jnp.where(
        is_image, type_table[1][None, :], type_table[0][None, :]
    )
    normed1_full, norm1_pull = jax.vjp(norm_rows, embedded, norm_gains[0], biases[0])
    normed1 = normed1_full.astype(jnp.bfloat16)
    group_normed = group_rows(normed1)
    head_offset = narrow_index * head_cols
    bias_query = lax.dynamic_slice_in_dim(biases[1], head_offset, head_cols)
    bias_value = lax.dynamic_slice_in_dim(biases[2], head_offset, head_cols)
    bias_stack = jnp.stack([bias_query, jnp.zeros_like(bias_query), bias_value])
    projected = jnp.einsum(
        "rd,sde->sre", group_normed, qkv_full, preferred_element_type=jnp.float32
    )
    qkv_rows = (projected + bias_stack[:, None, :]).astype(jnp.bfloat16)
    qkv_packs = qkv_rows.reshape(3, pack_count, pack_rows, heads_here, HD)
    attended, log_totals = lax.map(
        pack_forward, (qkv_packs[0], qkv_packs[1], qkv_packs[2], segment_ids)
    )
    attended = attended.reshape(group_count, head_cols)

    def out_term(first_row, row_span):
        return jnp.dot(attended, out_rows, preferred_element_type=jnp.float32)

    attn_proj = group_sums(out_term, local_rows)
    hidden1 = embedded + attn_proj + biases[3]
    normed2_full, norm2_pull = jax.vjp(norm_rows, hidden1, norm_gains[1], biases[4])
    normed2 = normed2_full.astype(jnp.bfloat16)
    mlp_input, mlp_back = (normed2, cotangent)
    pre_act = jnp.dot(mlp_input, up_cols, preferred_element_type=jnp.float32) + up_bias_cols.astype(
        jnp.float32
    )
    activated, gelu_pull = jax.vjp(gelu_exact, pre_act)
    act_low = activated.astype(jnp.bfloat16)
    mlp_out = jnp.dot(act_low, down_rows, preferred_element_type=jnp.float32)
    activations = (hidden1 + mlp_out + biases[5]).astype(jnp.bfloat16)
    grad_act = times_transposed(mlp_back, down_rows)
    (grad_pre,) = gelu_pull(grad_act)
    grad_pre_low = grad_pre.astype(jnp.bfloat16)
    grad_down = transposed_times(act_low, mlp_back)
    grad_up = transposed_times(mlp_input, grad_pre_low)
    grad_up_bias = jnp.sum(grad_pre_low.astype(jnp.float32), axis=0)
    grad_normed2 = times_transposed(grad_pre_low, up_cols)
    grad_hidden_part, grad_gain2, grad_shift2 = norm2_pull(grad_normed2)
    cotangent_full = cotangent.astype(jnp.float32)
    grad_hidden = cotangent_full + grad_hidden_part
    grad_hidden_low = grad_hidden.astype(jnp.bfloat16)
    group_back = group_rows(grad_hidden_low)
    grad_attended = times_transposed(group_back, out_rows).astype(jnp.bfloat16)
    grad_out_weight = transposed_times(attended, group_back)
    back_packs = grad_attended.reshape(pack_count, pack_rows, heads_here, HD)
    grad_queries, grad_keys, grad_values = lax.map(
        pack_backward,
        (qkv_packs[0], qkv_packs[1], qkv_packs[2], segment_ids, log_totals, back_packs),
    )
    grad_qkv_rows = jnp.stack([grad_queries, grad_keys, grad_values]).reshape(
        3, group_count, head_cols
    )
    grad_qkv_weight = jnp.einsum(
        "rd,sre->sde", group_normed, grad_qkv_rows, preferred_element_type=jnp.float32
    )
    head_sums = jnp.sum(grad_qkv_rows.astype(jnp.float32), axis=1)

    def in_term(first_row, row_span):
        return jnp.einsum(
            "sre,sde->rd", grad_qkv_rows, qkv_full, preferred_element_type=jnp.float32
        )

    grad_normed1 = group_sums(in_term, local_rows)
    grad_embed_part, grad_gain1, grad_shift1 = norm1_pull(grad_normed1)
    input_grad = grad_hidden + grad_embed_part
    zero_row = jnp.zeros((model_width,), jnp.float32)
    query_sums = lax.dynamic_update_slice_in_dim(zero_row, head_sums[0], head_offset, 0)
    value_sums = lax.dynamic_update_slice_in_dim(zero_row, head_sums[2], head_offset, 0)
    gain_part = jnp.stack([grad_gain1, grad_gain2])
    shift_part = jnp.stack(
        [
            grad_shift1,
            query_sums,
            value_sums,
            jnp.sum(grad_hidden, axis=0),
            grad_shift2,
            jnp.sum(cotangent_full, axis=0),
        ]
    )
    type_part = jnp.stack(
        [
            jnp.sum(jnp.where(is_image, 0.0, input_grad), axis=0),
            jnp.sum(jnp.where(is_image, input_grad, 0.0), axis=0),
        ]
    )
    grad_gains, grad_biases, grad_types = lax.psum(
        (gain_part, shift_part, type_part), ("wide", "narrow")
    )
    owned_qkv, owned_out = (
        sent_and_summed(grad_qkv_weight.astype(jnp.bfloat16), "wide", 1),
        sent_and_summed(grad_out_weight.astype(jnp.bfloat16), "wide", 1),
    )
    owned_up, owned_up_bias, owned_down = (
        lax.psum_scatter(grad_up, ("wide", "narrow"), scatter_dimension=1, tiled=True),
        lax.psum_scatter(grad_up_bias, ("wide", "narrow"), scatter_dimension=0, tiled=True),
        lax.psum_scatter(grad_down, ("wide", "narrow"), scatter_dimension=0, tiled=True),
    )
    step_sizes = step_rates()
    new_type = adam_update(type_table, type_first, type_second, grad_types, step_sizes[0])
    new_gains = adam_update(norm_gains, gains_first, gains_second, grad_gains, step_sizes[1])
    new_biases = adam_update(biases, biases_first, biases_second, grad_biases, step_sizes[2])
    new_qkv = adam_update(qkv_weight, qkv_first, qkv_second, owned_qkv, step_sizes[3])
    new_out = adam_update(out_weight, out_first, out_second, owned_out, step_sizes[4])
    new_up = adam_update(up_weight, up_first, up_second, owned_up, step_sizes[5])
    new_up_bias = adam_update(up_bias, up_bias_first, up_bias_second, owned_up_bias, step_sizes[6])
    new_down = adam_update(down_weight, down_first, down_second, owned_down, step_sizes[7])
    return (
        activations,
        input_grad,
        new_type[0],
        new_type[1],
        new_type[2],
        new_gains[0],
        new_gains[1],
        new_gains[2],
        new_biases[0],
        new_biases[1],
        new_biases[2],
        new_qkv[0],
        new_qkv[1],
        new_qkv[2],
        new_out[0],
        new_out[1],
        new_out[2],
        new_up[0],
        new_up[1],
        new_up[2],
        new_up_bias[0],
        new_up_bias[1],
        new_up_bias[2],
        new_down[0],
        new_down[1],
        new_down[2],
    )


def solution(mesh):
    placed = (
        P(("wide", "narrow"), None),
        P(("wide", "narrow")),
        P("wide", None),
        P(("wide", "narrow"), None),
        P(),
        P(),
        P(),
        P(),
        P(),
        P(),
        P(),
        P(),
        P(),
        P(None, "wide", "narrow"),
        P(None, "wide", "narrow"),
        P(None, "wide", "narrow"),
        P("narrow", "wide"),
        P("narrow", "wide"),
        P("narrow", "wide"),
        P(None, ("wide", "narrow")),
        P(None, ("wide", "narrow")),
        P(None, ("wide", "narrow")),
        P(("wide", "narrow")),
        P(("wide", "narrow")),
        P(("wide", "narrow")),
        P(("wide", "narrow"), None),
        P(("wide", "narrow"), None),
        P(("wide", "narrow"), None),
    )
    return jax.shard_map(
        shards,
        mesh=mesh,
        in_specs=placed,
        out_specs=(
            P(("wide", "narrow"), None),
            P(("wide", "narrow"), None),
            P(),
            P(),
            P(),
            P(),
            P(),
            P(),
            P(),
            P(),
            P(),
            P(None, "wide", "narrow"),
            P(None, "wide", "narrow"),
            P(None, "wide", "narrow"),
            P("narrow", "wide"),
            P("narrow", "wide"),
            P("narrow", "wide"),
            P(None, ("wide", "narrow")),
            P(None, ("wide", "narrow")),
            P(None, ("wide", "narrow")),
            P(("wide", "narrow")),
            P(("wide", "narrow")),
            P(("wide", "narrow")),
            P(("wide", "narrow"), None),
            P(("wide", "narrow"), None),
            P(("wide", "narrow"), None),
        ),
        check_vma=False,
    )
```

profile of v0, /device:TPU:0, one launch (start us, length us, event | category | flops | bytes accessed | tf_op | source)
XLA Modules:
  0.0 673.5 jit_solution(8733784257186419925)
XLA Ops:
  14.1 2.3 add_convert_fusion.3
  16.7 39.0 %all_gather.22 = bf16[3,768,192]{2,0,1:T(4,128)(2,1)S(1)} all-gather(bf16[3,96,192]{2,0,1:T(4,128)(2,1)S(1)} %copy.120), channel_id=1, replica_groups=mesh['wide'=8,'narrow'=4] {'wide'}, dimensions={1}, use_global_device_ids=true | all-gather | bytes 995328 | tf_op jit(solution)/shard_map/all_gather | solution.py:169
  56.8 31.2 %all_gather.23 = bf16[192,768]{0,1:T(8,128)(2,1)S(1)} all-gather(bf16[192,96]{0,1:T(8,128)(2,1)S(1)} %copy.126), channel_id=1, replica_groups=mesh['wide'=8,'narrow'=4] {'wide'}, dimensions={1}, use_global_device_ids=true | all-gather | bytes 331776 | tf_op jit(solution)/shard_map/all_gather | solution.py:170
  88.1 3.3 fusion.106
  97.2 12.4 %while.26 = (s32[]{:T(128)}, bf16[3,512,3,64]{1,3,2,0:T(8,128)(2,1)S(1)}, f32[3,3,512]{2,1,0:T(4,128)}, bf16[3,512,3,64]{1,3,2,0:T(8,128)(2,1)S(1)}, s32[3,512]{...) while((s32[]{:T(128)}, ...), condition=%wide.region_5.6_spmd, body=%wide.region_2.5_spmd.sunk | while | flops 211122688 | bytes 11335781 | solution.py:193
  110.2 2.3 convolution_convert_fusion
  115.3 39.1 %all-reduce = bf16[3072]{0:T(1024)(128)(2,1)S(1)} all-reduce(bf16[3072]{0:T(1024)(128)(2,1)S(1)} %dynamic-update-slice), channel_id=1, replica_groups=mesh['wide'=8,'narrow'=4] {'wide','narrow'}, use_global_device_ids=true, to_apply=%add | all-reduce | flops 3072 | bytes 12288
  156.0 1.6 multiply_reduce_fusion.3
  157.7 22.1 %all-gather.7.cloned.1.call-done = bf16[768,3072]{0,1:T(8,128)(2,1)} async-done(((bf16[768,96]{0,1:T(8,128)(2,1)}), bf16[768,3072]{0,1:T(8,128)(2,1)}) %all-gather.7.cloned.1.call-update) | async-done | bytes 4718608 | tf_op jit(solution)/shard_map/all_gather | solution.py:173
  179.8 7.0 %convolution_add_fusion = f32[384,3072]{1,0:T(8,128)} fusion(bf16[768,3072]{0,1:T(8,128)(2,1)} %all-gather.7.cloned.1.call-done, f32[3072]{0:T(1024)S(1)} %convert_element_type.128, f32[768]{0:T(1024)} %get-tuple-element.344, f32[768]{0:T(1024)S(1)} %get-tuple-element.261, f32[384]{0:T(512)S(1)} %fusion.87, f32[384]{0:T(512)S(1)} %broadcast_multiply_fusion, ...), kind=kOutput, calls=%fused_computation.81 | convolution fusion | flops 1816363008 | bytes 10647936 | tf_op jit(solution)/shard_map/dot_general | solution.py:206
  186.8 58.8 %all-gather.9.cloned.1.call-done = bf16[3072,768]{1,0:T(8,128)(2,1)} async-done(((bf16[96,768]{1,0:T(8,128)(2,1)}), bf16[3072,768]{1,0:T(8,128)(2,1)}) %all-gather.9.cloned.1.call-update) | async-done | bytes 4718608 | tf_op jit(solution)/shard_map/all_gather | solution.py:175
  245.6 16.1 %convert_reduce_fusion = (f32[3072]{0:T(1024)}, bf16[384,3072]{1,0:T(8,128)(2,1)S(1)}, f32[384,3072]{1,0:T(8,128)}) fusion(f32[384,3072]{1,0:T(8,128)} %convolution_add_fusion, bf16[384,768]{1,0:T(8,128)(2,1)S(1)} %copy-done.4, bf16[3072,768]{1,0:T(8,128)(2,1)} %all-gather.9.cloned.1.call-done), kind=kOutput, calls=%fused_computation.65 | convolution fusion | flops 1899230208 | bytes 17117184 | tf_op jit(solution)/shard_map/dot_general | solution.py:40
  261.8 2.8 multiply_reduce_fusion.1
  267.4 22.3 %all-gather.11.cloned.1.call-done = bf16[1536,768]{1,0:T(8,128)(2,1)} async-done(((bf16[384,768]{1,0:T(8,128)(2,1)}), bf16[1536,768]{1,0:T(8,128)(2,1)}) %all-gather.11.cloned.1.call-update) | async-done | bytes 2359312 | tf_op jit(solution)/shard_map/all_gather | solution.py:64
  289.7 3.4 convolution_convert_fusion.1
  293.1 2.1 reshape.248
  299.2 26.4 %while.27 = (s32[]{:T(128)}, bf16[3,512,3,64]{1,3,2,0:T(8,128)(2,1)}, bf16[3,512,3,64]{1,3,2,0:T(8,128)(2,1)}, bf16[3,512,3,64]{1,3,2,0:T(8,128)(2,1)}, bf16[3,5...) while((s32[]{:T(128)}, ...), condition=%wide.region_13.14_spmd, body=%wide.region_11.13_spmd.sunk | while | flops 511146496 | bytes 26127484 | solution.py:228
  329.8 2.5 copy.132
  332.3 2.5 stack.46
  334.8 2.5 copy.133
  337.3 2.6 stack.47
  343.3 3.4 bitcast_convert_fusion
  347.9 8.6 %fusion.91 = f32[768,3072]{0,1:T(8,128)} fusion(bf16[384,3072]{1,0:T(8,128)(2,1)} %copy-done.13, f32[768]{0:T(1024)S(1)} %copy-done.32, f32[768]{0:T(1024)S(1)} %get-tuple-element.261, f32[384]{0:T(512)S(1)} %copy-done.47, f32[384]{0:T(512)S(1)} %copy-done.45, bf16[384,768]{1,0:T(8,128)(2,1)S(1)} %copy-done.3, bf16[384,768]{1,0:T(8,128)(2,1)S(1)} %copy-done, ...), kind=kOutput, calls=%fused_computation.186 | convolution fusion | flops 1815183360 | bytes 12994944 | tf_op jit(solution)/shard_map/dot_general | solution.py:46
  356.5 4.9 multiply_convert_fusion.1
  363.0 5.1 fusion.107
  369.1 3.0 convolution_convert_fusion.2
  374.4 5.5 all-to-all-start.1
  379.9 4.6 fusion.70
  384.5 3.2 reshape.253
  387.7 2.6 copy.153
  390.3 1.7 all-to-all-done.1
  392.0 4.8 all-to-all-start
  396.8 1.8 copy.140
  398.6 1.8 copy.135
  400.5 1.8 copy.138
  403.5 6.4 fusion.69
  411.2 1.8 multiply_subtract_fusion.3
  412.9 12.3 %all-to-all-done = bf16[8,3,96,192]{2,3,1,0:T(8,128)(2,1)} async-done(((bf16[8,3,96,192]{2,3,1,0:T(8,128)(2,1)}), bf16[8,3,96,192]{2,3,1,0:T(8,128)(2,1)}, u32[]{:S(2)}, u32[]{:S(2)}) %all-to-all-start) | async-done | bytes 884768 | tf_op jit(solution)/shard_map/all_to_all | solution.py:24
  428.0 1.9 copy.142
  429.8 1.8 copy.143
  432.6 1.7 convert_reduce_fusion.3
  434.3 1.9 fusion.74
  436.5 2.8 convert_reduce_fusion.4
  439.5 40.1 %all-reduce.2 = (f32[2,768]{1,0:T(2,128)S(1)}, f32[2,768]{1,0:T(2,128)S(1)}, f32[6,768]{1,0:T(8,128)S(1)}, f32[3072]{0:T(1024)S(1)}) all-reduce(f32[2,768]{1,0:T(2,128)S(1)} %pad_maximum_fusion, f32[2,768]{1,0:T(2,128)S(1)} %pad_maximum_fusion.1, f32[6,768]{1,0:T(8,128)S(1)} %stack.55, ...), channel_id=1, replica_groups=mesh['wide'=8,'narrow'=4] {'wide','narrow'}, use_global_device_ids=true, to_apply=%region_19.20 | all-reduce | flops 10752 | bytes 86016 | tf_op jit(solution)/shard_map/psum | solution.py:268
  482.2 40.1 %reduce-scatter.9.cloned.1.call-done = f32[768,96]{0,1:T(8,128)} async-done(((f32[768,3072]{0,1:T(8,128)}), f32[768,96]{0,1:T(8,128)}) %reduce-scatter.9.cloned.1.call-update) | async-done | bytes 294928 | tf_op jit(solution)/shard_map/reduce_scatter | solution.py:276
  522.3 2.0 multiply_subtract_fusion.1
  524.4 139.2 %reduce-scatter.11.cloned.1.call-done = f32[96,768]{1,0:T(8,128)} async-done(((f32[3072,768]{1,0:T(8,128)}), f32[96,768]{1,0:T(8,128)}) %reduce-scatter.11.cloned.1.call-update) | async-done | bytes 294928 | tf_op jit(solution)/shard_map/reduce_scatter | solution.py:278
  663.6 2.0 multiply_subtract_fusion
  (293 shorter events, 85.8 us)
Async XLA Ops:
  8.0 80.0 %all-gather.5.cloned.1.call-start = ((), (), s32[]{:S(2)}) async-start(), calls=%async_computation.6 | async-start | bytes 2949120 | tf_op jit(solution)/shard_map/all_gather | solution.py:64
  16.4 138.0 %reduce-scatter.5.cloned.1.call-start = ((), (), s32[]{:S(2)}) async-start(), calls=%async_computation.7 | async-start | bytes 2949120 | tf_op jit(solution)/shard_map/reduce_scatter | solution.py:68
  16.7 39.9 %copy-start.26 = (f32[192,96]{1,0:T(8,128)S(1)}, f32[192,96]{1,0:T(8,128)}, u32[]{:S(2)}) copy-start(f32[192,96]{1,0:T(8,128)} %param.48) | copy-start | bytes 221188
  56.6 34.8 %copy-start.24 = (bf16[3,768,192]{1,2,0:T(8,128)(2,1)}, bf16[3,768,192]{1,2,0:T(8,128)(2,1)S(1)}, u32[]{:S(2)}) copy-start(bf16[3,768,192]{1,2,0:T(8,128)(2,1)S(1)} %copy.121) | copy-start | bytes 2654212
  88.0 22.2 %copy-start.9 = (bf16[192,768]{0,1:T(8,128)(2,1)}, bf16[192,768]{0,1:T(8,128)(2,1)S(1)}, u32[]{:S(2)}) copy-start(bf16[192,768]{0,1:T(8,128)(2,1)S(1)} %all_gather.23) | copy-start | bytes 884740
  112.6 41.8 %copy-start = (bf16[384,768]{1,0:T(8,128)(2,1)S(1)}, bf16[384,768]{1,0:T(8,128)(2,1)}, u32[]{:S(2)}) copy-start(bf16[384,768]{1,0:T(8,128)(2,1)} %param.32) | copy-start | bytes 1769476
  112.6 41.8 %copy-start.36 = (pred[384]{0:T(512)(128)(4,1)S(1)}, pred[384]{0:T(512)(128)(4,1)}, u32[]{:S(2)}) copy-start(pred[384]{0:T(512)(128)(4,1)} %copy-done.35) | copy-start | bytes 1156
  112.6 67.2 %all-gather.7.cloned.1.call-start = ((), (), s32[]{:S(2)}) async-start(), calls=%async_computation.8 | async-start | bytes 4866048 | tf_op jit(solution)/shard_map/all_gather | solution.py:173
  114.2 131.4 %all-gather.9.cloned.1.call-start = ((), (), s32[]{:S(2)}) async-start(), calls=%async_computation.9 | async-start | bytes 4866048 | tf_op jit(solution)/shard_map/all_gather | solution.py:175
  115.0 174.7 %all-gather.11.cloned.1.call-start = ((), (), s32[]{:S(2)}) async-start(), calls=%async_computation.10 | async-start | bytes 2949120 | tf_op jit(solution)/shard_map/all_gather | solution.py:64
  154.4 25.4 %copy-start.2 = (bf16[384,768]{1,0:T(8,128)(2,1)S(1)}, bf16[384,768]{1,0:T(8,128)(2,1)}, u32[]{:S(2)}) copy-start(bf16[384,768]{1,0:T(8,128)(2,1)} %reduce-scatter.5.cloned.1.call-done) | copy-start | bytes 1769476
  156.0 105.7 %copy-start.44 = (f32[384]{0:T(512)}, f32[384]{0:T(512)S(1)}, u32[]{:S(2)}) copy-start(f32[384]{0:T(512)S(1)} %broadcast_multiply_fusion) | copy-start | bytes 4612
  157.7 104.1 %copy-start.46 = (f32[384]{0:T(512)}, f32[384]{0:T(512)S(1)}, u32[]{:S(2)}) copy-start(f32[384]{0:T(512)S(1)} %fusion.87) | copy-start | bytes 4612
  179.8 65.8 %copy-start.4 = (bf16[384,768]{1,0:T(8,128)(2,1)S(1)}, bf16[384,768]{1,0:T(8,128)(2,1)}, u32[]{:S(2)}) copy-start(bf16[384,768]{1,0:T(8,128)(2,1)} %param.35) | copy-start | bytes 1769476
  186.8 75.0 %copy-start.37 = (pred[384]{0:T(512)(128)(4,1)S(1)}, pred[384]{0:T(512)(128)(4,1)}, u32[]{:S(2)}) copy-start(pred[384]{0:T(512)(128)(4,1)} %copy-done.35) | copy-start | bytes 1156
  245.6 16.2 %copy-start.75 = (bf16[768,3072]{0,1:T(8,128)(2,1)S(1)}, bf16[768,3072]{0,1:T(8,128)(2,1)}, u32[]{:S(2)}) copy-start(bf16[768,3072]{0,1:T(8,128)(2,1)} %all-gather.7.cloned.1.call-done) | copy-start | bytes 14155780
  266.1 23.6 %copy-start.10 = (bf16[192,768]{0,1:T(8,128)(2,1)S(1)}, bf16[192,768]{0,1:T(8,128)(2,1)}, u32[]{:S(2)}) copy-start(bf16[192,768]{0,1:T(8,128)(2,1)} %copy-done.9) | copy-start | bytes 884740
  266.2 27.0 %copy-start.56 = (f32[384]{0:T(512)}, f32[384]{0:T(512)S(1)}, u32[]{:S(2)}) copy-start(f32[384]{0:T(512)S(1)} %negate_multiply_fusion.2) | copy-start | bytes 4612
  267.2 165.3 %reduce-scatter.7.cloned.1.call-start = ((), (), s32[]{:S(2)}) async-start(), calls=%async_computation.11 | async-start | bytes 2949120 | tf_op jit(solution)/shard_map/reduce_scatter | solution.py:68
  346.8 175.5 %reduce-scatter.9.cloned.1.call-start = ((), (), s32[]{:S(2)}) async-start(), calls=%async_computation.12 | async-start | bytes 9732096 | tf_op jit(solution)/shard_map/reduce_scatter | solution.py:276
  356.5 307.1 %reduce-scatter.11.cloned.1.call-start = ((), (), s32[]{:S(2)}) async-start(), calls=%async_computation.13 | async-start | bytes 9732096 | tf_op jit(solution)/shard_map/reduce_scatter | solution.py:278
  374.4 17.7 %all-to-all-start.1 = ((bf16[8,192,96]{2,1,0:T(8,128)(2,1)}), bf16[8,192,96]{2,1,0:T(8,128)(2,1)S(1)}, u32[]{:S(2)}, u32[]{:S(2)}) async-start(bf16[8,192,96]{2,1,0:T(8,128)(2,1)} %bitcast.132), calls=%async_computation.3 | async-start | bytes 786432 | tf_op jit(solution)/shard_map/all_to_all | solution.py:24
  392.0 10.9 %copy-start.69 = (f32[768]{0:T(1024)S(1)}, f32[768]{0:T(1024)}, u32[]{:S(2)}) copy-start(f32[768]{0:T(1024)} %get-tuple-element.249) | copy-start | bytes 9220
  392.0 11.5 %copy-start.40 = (pred[384]{0:T(512)(128)(4,1)S(1)}, pred[384]{0:T(512)(128)(4,1)}, u32[]{:S(2)}) copy-start(pred[384]{0:T(512)(128)(4,1)} %copy-done.35) | copy-start | bytes 1156
  392.0 11.5 %copy-start.68 = (f32[768]{0:T(1024)S(1)}, f32[768]{0:T(1024)}, u32[]{:S(2)}) copy-start(f32[768]{0:T(1024)} %get-tuple-element.345) | copy-start | bytes 9220
  392.0 33.3 %all-to-all-start = ((bf16[8,3,96,192]{2,3,1,0:T(8,128)(2,1)}), bf16[8,3,96,192]{2,3,1,0:T(8,128)(2,1)}, u32[]{:S(2)}, u32[]{:S(2)}) async-start(bf16[8,3,96,192]{2,3,1,0:T(8,128)(2,1)} %bitcast.173), calls=%async_computation.2 | async-start | bytes 2359296 | tf_op jit(solution)/shard_map/all_to_all | solution.py:24
  410.2 16.7 %copy-start.21 = (f32[3,96,192]{1,2,0:T(8,128)S(1)}, f32[3,96,192]{1,2,0:T(8,128)}, u32[]{:S(2)}) copy-start(f32[3,96,192]{1,2,0:T(8,128)} %copy.140) | copy-start | bytes 663556
  410.2 16.7 %copy-start.22 = (f32[3,96,192]{1,2,0:T(8,128)S(1)}, f32[3,96,192]{1,2,0:T(8,128)}, u32[]{:S(2)}) copy-start(f32[3,96,192]{1,2,0:T(8,128)} %copy.135) | copy-start | bytes 663556
  411.1 14.2 %copy-start.60 = (f32[1,768]{1,0:T(1,128)}, f32[1,768]{1,0:T(1,128)S(1)}, u32[]{:S(2)}) copy-start(f32[1,768]{1,0:T(1,128)S(1)} %dynamic_update_slice.26) | copy-start | bytes 9220
  411.2 15.8 %copy-start.23 = (f32[3,96,192]{1,2,0:T(8,128)S(1)}, f32[3,96,192]{1,2,0:T(8,128)}, u32[]{:S(2)}) copy-start(f32[3,96,192]{1,2,0:T(8,128)} %copy.138) | copy-start | bytes 663556
  436.3 43.3 %copy-start.72 = (f32[96]{0:T(128)S(1)}, f32[96]{0:T(128)}, u32[]{:S(2)}) copy-start(f32[96]{0:T(128)} %param.54) | copy-start | bytes 1156
  436.3 43.3 %copy-start.73 = (f32[96]{0:T(128)S(1)}, f32[96]{0:T(128)}, u32[]{:S(2)}) copy-start(f32[96]{0:T(128)} %param.55) | copy-start | bytes 1156
  436.3 43.3 %copy-start.74 = (f32[96]{0:T(128)S(1)}, f32[96]{0:T(128)}, u32[]{:S(2)}) copy-start(f32[96]{0:T(128)} %param.56) | copy-start | bytes 1156
  436.4 44.0 %copy-start.50 = (f32[2,768]{1,0:T(2,128)S(1)}, f32[2,768]{1,0:T(2,128)}, u32[]{:S(2)}) copy-start(f32[2,768]{1,0:T(2,128)} %param.36) | copy-start | bytes 18436
  436.4 43.9 %copy-start.64 = (f32[2,768]{1,0:T(2,128)S(1)}, f32[2,768]{1,0:T(2,128)}, u32[]{:S(2)}) copy-start(f32[2,768]{1,0:T(2,128)} %param.37) | copy-start | bytes 18436
  436.4 43.9 %copy-start.65 = (f32[2,768]{1,0:T(2,128)S(1)}, f32[2,768]{1,0:T(2,128)}, u32[]{:S(2)}) copy-start(f32[2,768]{1,0:T(2,128)} %param.38) | copy-start | bytes 18436
  436.4 44.6 %copy-start.51 = (f32[2,768]{1,0:T(2,128)S(1)}, f32[2,768]{1,0:T(2,128)}, u32[]{:S(2)}) copy-start(f32[2,768]{1,0:T(2,128)} %param.39) | copy-start | bytes 18436
  436.4 44.5 %copy-start.66 = (f32[2,768]{1,0:T(2,128)S(1)}, f32[2,768]{1,0:T(2,128)}, u32[]{:S(2)}) copy-start(f32[2,768]{1,0:T(2,128)} %param.40) | copy-start | bytes 18436
  436.4 44.5 %copy-start.67 = (f32[2,768]{1,0:T(2,128)S(1)}, f32[2,768]{1,0:T(2,128)}, u32[]{:S(2)}) copy-start(f32[2,768]{1,0:T(2,128)} %param.41) | copy-start | bytes 18436
  436.4 45.2 %copy-start.41 = (f32[6,768]{1,0:T(8,128)S(1)}, f32[6,768]{1,0:T(8,128)}, u32[]{:S(2)}) copy-start(f32[6,768]{1,0:T(8,128)} %param.42) | copy-start | bytes 55300
  436.4 45.1 %copy-start.52 = (f32[6,768]{1,0:T(8,128)S(1)}, f32[6,768]{1,0:T(8,128)}, u32[]{:S(2)}) copy-start(f32[6,768]{1,0:T(8,128)} %param.43) | copy-start | bytes 55300
  436.5 45.1 %copy-start.53 = (f32[6,768]{1,0:T(8,128)S(1)}, f32[6,768]{1,0:T(8,128)}, u32[]{:S(2)}) copy-start(f32[6,768]{1,0:T(8,128)} %param.44) | copy-start | bytes 55300
  436.5 85.9 %copy-start.18 = (f32[768,96]{0,1:T(8,128)S(1)}, f32[768,96]{0,1:T(8,128)}, u32[]{:S(2)}) copy-start(f32[768,96]{0,1:T(8,128)} %param.51) | copy-start | bytes 884740
  436.5 85.9 %copy-start.28 = (f32[768,96]{0,1:T(8,128)S(1)}, f32[768,96]{0,1:T(8,128)}, u32[]{:S(2)}) copy-start(f32[768,96]{0,1:T(8,128)} %param.52) | copy-start | bytes 884740
  436.5 85.9 %copy-start.29 = (f32[768,96]{0,1:T(8,128)S(1)}, f32[768,96]{0,1:T(8,128)}, u32[]{:S(2)}) copy-start(f32[768,96]{0,1:T(8,128)} %param.53) | copy-start | bytes 884740
  439.3 224.3 %copy-start.20 = (f32[96,768]{1,0:T(8,128)S(1)}, f32[96,768]{1,0:T(8,128)}, u32[]{:S(2)}) copy-start(f32[96,768]{1,0:T(8,128)} %param.57) | copy-start | bytes 884740
  439.3 224.3 %copy-start.30 = (f32[96,768]{1,0:T(8,128)S(1)}, f32[96,768]{1,0:T(8,128)}, u32[]{:S(2)}) copy-start(f32[96,768]{1,0:T(8,128)} %param.58) | copy-start | bytes 884740
  439.3 224.3 %copy-start.31 = (f32[96,768]{1,0:T(8,128)S(1)}, f32[96,768]{1,0:T(8,128)}, u32[]{:S(2)}) copy-start(f32[96,768]{1,0:T(8,128)} %param.59) | copy-start | bytes 884740
  (38 other events, 126.3 us)
Sparse Core Ops, SparseCore 0:
  16.5 26.7 all-gather.4
  112.7 32.7 reduce-scatter.4
  267.3 22.3 all-gather.10
  347.0 33.0 reduce-scatter.6
  385.8 136.4 reduce-scatter.8
  529.1 134.4 reduce-scatter.10
Sparse Core Ops, SparseCore 1:
  116.6 63.1 all-gather.6
  183.6 62.0 all-gather.8
where the time goes:
time: 683 us; the launch traced here: 673 us
  waiting for transfers between devices  297 us (43%)
  blocking collectives  149 us (22%)
  matrix products  90.7 us (13%)
  local copies, waits for them, and re-layouts  64.8 us (9%)
  other arithmetic  43.8 us (6%)
  between operations  17.1 us (3%)
  starting transfers between devices  11 us (2%)
    reduce_scatter x1, waiting for transfers between devices, shards(): lax.psum_scatter(grad_down, ('wide', 'narrow'), scatter_dimension=0, tile...  139 us
    all_gather x1, waiting for transfers between devices, shards(): lax.all_gather(down_low, ('wide', 'narrow'), axis=0, tiled=True)  58.8 us
    psum x1, blocking collectives, shards(): lax.psum((gain_part, shift_part, type_part), ('wide', 'narrow'))  40.1 us
    reduce_scatter x1, waiting for transfers between devices, shards(): lax.psum_scatter(grad_up, ('wide', 'narrow'), scatter_dimension=1, tiled=...  40.1 us
    unnamed x1, blocking collectives  39.1 us
    all_gather x1, blocking collectives, shards(): lax.all_gather(qkv_low, 'wide', axis=1, tiled=True)  39 us
    all_gather x1, blocking collectives, shards(): lax.all_gather(out_low, 'wide', axis=1, tiled=True)  31.2 us
    dot_general x3, matrix products, times_transposed(): lax.dot_general(left_mat, right_mat, (((1,), (1,)), ((), ())), preferred_...  22.3 us
  transfers between devices with their start and end apart: 10, of which 7 were waited for; matrix products, arithmetic and copies ran while one was open for 12% of the time, Pallas kernels for 0%

commit v1 on v0

--- a/solution.py
+++ b/solution.py
@@ -1,6 +1,10 @@
+import math
+
 import jax
 import jax.numpy as jnp
 from jax import lax
+from jax.experimental import pallas as pl
+from jax.experimental.pallas import tpu as pltpu
 from jax.sharding import PartitionSpec as P
 
 D = 768
@@ -316,6 +320,764 @@
     )
 
 
+def dot_nn(left_mat, right_mat):
+    return lax.dot_general(
+        left_mat, right_mat, (((1,), (0,)), ((), ())), preferred_element_type=jnp.float32
+    )
+
+
+def dot_nt(left_mat, right_mat):
+    return lax.dot_general(
+        left_mat, right_mat, (((1,), (1,)), ((), ())), preferred_element_type=jnp.float32
+    )
+
+
+def dot_tn(left_mat, right_mat):
+    return lax.dot_general(
+        left_mat, right_mat, (((0,), (0,)), ((), ())), preferred_element_type=jnp.float32
+    )
+
+
+def rows_at(block, size):
+    return pl.ds(pl.multiple_of(block * size, size), size)
+
+
+def row_stats(values):
+    center = jnp.mean(values, axis=-1, keepdims=True)
+    spread = values - center
+    variance = jnp.mean(spread * spread, axis=-1, keepdims=True)
+    scale = lax.rsqrt(variance + norm_eps)
+    return spread * scale, scale
+
+
+def column_sums(values):
+    return jnp.sum(values, axis=0, keepdims=True)
+
+
+ROW = 128
+OWN = 384
+CHIP = 768
+HALF_PACK = 256
+PACK = 512
+BLK = 96
+HALF_BLK = 48
+ATTN, UP, DOWN = 0, 1, 2
+GAIN_ROW, BIAS_ROW, TYPE_ROW, UP_BIAS_ROW, SMALL_ROWS = 0, 2, 8, 10, 16
+
+
+def layer_kernel(
+    own, unit_bias, tokens, is_image, cotangent, query_doc, key_doc, type_table, gains, biases, qkv_bias,
+    act_out, input_grad, grad_out, small_out,
+    full, part, g_all, n1_all, n2_all, dh_all, qkv, att, dkv_far, probs, mask, act, slope, datt,
+    key_acc, value_acc, embedded, hidden1, own_sum, swap_send, swap_recv, bias_slots, bias_row, small,
+    small_recv, rx, ry, rdx, rdy, rz,
+    gz_s, gz_r, gx_s, gx_r, gy_s, gy_r, gfx_s, gfx_r, gfy_s, gfy_r,
+    sz_s, sz_r, sx_s, sx_r, sy_s, sy_r, sdx_s, sdx_r, sdy_s, sdy_r,
+    spread_s, spread_r, swap_s, swap_r, far_s, far_r, bias_s, bias_r, small_s, small_r,
+):
+    f32, bf16 = jnp.float32, jnp.bfloat16
+    wide = lax.axis_index("wide")
+    narrow = lax.axis_index("narrow")
+    z, x = wide // 2, wide % 2
+    y, core = narrow // 2, narrow % 2
+    z_of = [z, z + 1 - 2 * (z % 2), (z + 2) % 4, 3 - z]
+    sibling = (wide, y * 2 + (1 - core))
+    x_side = (z * 2 + (1 - x), narrow)
+    y_side = (wide, (1 - y) * 2 + core)
+    z_side = [None] + [(z_of[j] * 2 + x, narrow) for j in (1, 2, 3)]
+
+    def copy(src, dst, send, recv, to):
+        return pltpu.make_async_remote_copy(
+            src_ref=src, dst_ref=dst, send_sem=send, recv_sem=recv, device_id=to,
+            device_id_type=pl.DeviceIdType.MESH,
+        )
+
+    pending = []
+
+    def start(*args):
+        one = copy(*args)
+        one.start()
+        pending.append(one)
+        return one
+
+    barrier = pltpu.get_barrier_semaphore()
+    for to in (sibling, x_side, y_side, z_side[1], z_side[2], z_side[3]):
+        pl.semaphore_signal(barrier, inc=1, device_id=to, device_id_type=pl.DeviceIdType.MESH)
+    pl.semaphore_wait(barrier, 6)
+
+    def slot(ref, kind, yy, zz, xx, first=0, size=BLK):
+        row = pl.multiple_of((zz * 2 + xx) * BLK + first, 16)
+        return ref.at[kind, yy, pl.ds(row, size)]
+
+    def gather_z(kind):
+        mine = slot(full, kind, y, z, x)
+        for j in (1, 2, 3):
+            start(mine, mine, gz_s.at[kind, j], gz_r.at[kind, j], z_side[j])
+
+    def gather_on(kind, j):
+        block = slot(full, kind, y, z_of[j], x)
+        if j:
+            copy(block, block, gz_s.at[kind, j], gz_r.at[kind, j], z_side[j]).wait_recv()
+        start(block, block, gx_s.at[kind, j], gx_r.at[kind, j], x_side)
+        start(block, block, gy_s.at[kind, j], gy_r.at[kind, j], y_side)
+
+    def gather_far(kind, j):
+        zz = z_of[j]
+        block = slot(full, kind, y, zz, 1 - x)
+        copy(block, block, gx_s.at[kind, j], gx_r.at[kind, j], x_side).wait_recv()
+        half = slot(full, kind, y, zz, 1 - x, 0, HALF_BLK)
+        start(half, half, gfy_s.at[kind, j], gfy_r.at[kind, j], y_side)
+        block = slot(full, kind, 1 - y, zz, x)
+        copy(block, block, gy_s.at[kind, j], gy_r.at[kind, j], y_side).wait_recv()
+        half = slot(full, kind, 1 - y, zz, x, HALF_BLK, HALF_BLK)
+        start(half, half, gfx_s.at[kind, j], gfx_r.at[kind, j], x_side)
+
+    def gather_done(kind):
+        for j in range(4):
+            half = slot(full, kind, 1 - y, z_of[j], 1 - x, 0, HALF_BLK)
+            copy(half, half, gfy_s.at[kind, j], gfy_r.at[kind, j], y_side).wait_recv()
+            half = slot(full, kind, 1 - y, z_of[j], 1 - x, HALF_BLK, HALF_BLK)
+            copy(half, half, gfx_s.at[kind, j], gfx_r.at[kind, j], x_side).wait_recv()
+
+    def scatter_far(kind, j):
+        half = slot(part, kind, 1 - y, z_of[j], 1 - x, 0, HALF_BLK)
+        start(half, rdy.at[kind, j], sdy_s.at[kind, j], sdy_r.at[kind, j], y_side)
+        half = slot(part, kind, 1 - y, z_of[j], 1 - x, HALF_BLK, HALF_BLK)
+        start(half, rdx.at[kind, j], sdx_s.at[kind, j], sdx_r.at[kind, j], x_side)
+
+    def add_in(ref, arrived):
+        ref[...] = (ref[...].astype(f32) + arrived[...].astype(f32)).astype(bf16)
+
+    def scatter_near(kind, j):
+        zz = z_of[j]
+        half = slot(part, kind, y, zz, 1 - x, 0, HALF_BLK)
+        copy(half, rdy.at[kind, j], sdy_s.at[kind, j], sdy_r.at[kind, j], y_side).wait_recv()
+        add_in(half, rdy.at[kind, j])
+        start(slot(part, kind, y, zz, 1 - x), rx.at[kind, j], sx_s.at[kind, j], sx_r.at[kind, j], x_side)
+        half = slot(part, kind, 1 - y, zz, x, HALF_BLK, HALF_BLK)
+        copy(half, rdx.at[kind, j], sdx_s.at[kind, j], sdx_r.at[kind, j], x_side).wait_recv()
+        add_in(half, rdx.at[kind, j])
+        start(slot(part, kind, 1 - y, zz, x), ry.at[kind, j], sy_s.at[kind, j], sy_r.at[kind, j], y_side)
+
+    def scatter_z(kind, j):
+        block = slot(part, kind, y, z_of[j], x)
+        copy(block, rx.at[kind, j], sx_s.at[kind, j], sx_r.at[kind, j], x_side).wait_recv()
+        copy(block, ry.at[kind, j], sy_s.at[kind, j], sy_r.at[kind, j], y_side).wait_recv()
+        total = block[...].astype(f32) + rx[kind, j].astype(f32) + ry[kind, j].astype(f32)
+        if j:
+            block[...] = total.astype(bf16)
+            start(block, rz.at[kind, j], sz_s.at[kind, j], sz_r.at[kind, j], z_side[j])
+        else:
+            grad_out[kind] = total
+
+    def scatter_done(kind):
+        for j in (1, 2, 3):
+            copy(rz.at[kind, j], rz.at[kind, j], sz_s.at[kind, j], sz_r.at[kind, j], z_side[j]).wait_recv()
+        grad_out[kind] = grad_out[kind] + (
+            rz[kind, 1].astype(f32) + rz[kind, 2].astype(f32) + rz[kind, 3].astype(f32)
+        )
+
+    def place(which, block):
+        return rows_at((3 * which + block + 4 * y) % 6, ROW)
+
+    def hand_over(ref, use, block):
+        here = ref.at[place(core, block)]
+        return copy(here, here, spread_s.at[use, block], spread_r.at[use, block], sibling)
+
+    def spread_done(ref, use):
+        for block in range(3):
+            there = ref.at[place(1 - core, block)]
+            copy(there, there, spread_s.at[use, block], spread_r.at[use, block], sibling).wait_recv()
+            pending.append(hand_over(ref, use, block))
+
+    def swap_sums(use, term):
+        def for_sibling(block, carry):
+            rows = rows_at(block, ROW)
+            swap_send[use, rows] = term(place(1 - core, block)).astype(bf16)
+            copy(
+                swap_send.at[use, rows], swap_recv.at[use, rows], swap_s.at[use, block],
+                swap_r.at[use, block], sibling,
+            ).start()
+            return carry
+
+        def for_self(block, carry):
+            own_sum[rows_at(block, ROW)] = term(place(core, block))
+            return carry
+
+        lax.fori_loop(0, 3, for_sibling, 0)
+        lax.fori_loop(0, 3, for_self, 0)
+
+    def swap_done(use):
+        for block in range(3):
+            rows = pl.ds(block * ROW, ROW)
+            one = copy(
+                swap_send.at[use, rows], swap_recv.at[use, rows], swap_s.at[use, block],
+                swap_r.at[use, block], sibling,
+            )
+            one.wait_recv()
+            pending.append(one)
+
+    def swapped(use, rows):
+        return own_sum[rows] + swap_recv[use, rows].astype(f32)
+
+    for kind in (ATTN, UP, DOWN):
+        slot(full, kind, y, z, x)[...] = own[kind]
+    gather_z(ATTN)
+    gather_on(ATTN, 0)
+
+    def give_cotangent(block, carry):
+        g_all[place(core, block)] = cotangent[rows_at(block, ROW)]
+        hand_over(g_all, 0, block).start()
+        return carry
+
+    def first_norm(block, carry):
+        rows = rows_at(block, ROW)
+        values = tokens[rows].astype(f32) + jnp.where(
+            is_image[rows] > 0, type_table[1:2, :], type_table[0:1, :]
+        )
+        embedded[rows] = values
+        xhat, _ = row_stats(values)
+        n1_all[place(core, block)] = (xhat * gains[0:1, :] + biases[0:1, :]).astype(bf16)
+        hand_over(n1_all, 1, block).start()
+        return carry
+
+    lax.fori_loop(0, 3, first_norm, 0)
+
+    half_rows = pl.ds(PACK, HALF_PACK)
+    far_rows = pl.ds(CHIP, HALF_PACK)
+    over_y = copy(n1_all.at[half_rows], n1_all.at[far_rows], far_s.at[0], far_r.at[0], y_side)
+    relay = copy(n1_all.at[far_rows], n1_all.at[far_rows], far_s.at[1], far_r.at[1], sibling)
+    holds_half = (core + y) == 1
+
+    @pl.when(holds_half)
+    def _():
+        over_y.start()
+
+    def bias_hop(first, size, index, to):
+        ref = bias_slots.at[pl.ds(first, size)]
+        return start(ref, ref, bias_s.at[index], bias_r.at[index], to)
+
+    def bias_wait(first, size, index, to):
+        ref = bias_slots.at[pl.ds(first, size)]
+        copy(ref, ref, bias_s.at[index], bias_r.at[index], to).wait_recv()
+
+    bias_first = (y * 2 + x) * 4
+    bias_slots[bias_first + z] = unit_bias[...]
+    for j in (1, 2, 3):
+        bias_hop(bias_first + z, 1, j, z_side[j])
+
+    lax.fori_loop(0, 3, give_cotangent, 0)
+    gather_z(UP)
+
+    for tile in range(3):
+        rows = pl.ds(tile * 256, 256)
+        mask[rows] = jnp.where(
+            query_doc[rows] == key_doc[tile // 2 : tile // 2 + 1, :], 0.0, masked_score
+        ).astype(bf16)
+    small[...] = jnp.zeros_like(small)
+    for yy in (0, 1):
+        att[yy, :, 0:HD] = jnp.zeros((CHIP, HD), bf16)
+        qkv[yy, :, 576:768] = jnp.zeros((CHIP + HALF_PACK, 192), bf16)
+
+    gather_on(ATTN, 1)
+    gather_far(ATTN, 0)
+    gather_on(ATTN, 2)
+    gather_far(ATTN, 1)
+
+    @pl.when(jnp.logical_not(holds_half))
+    def _():
+        over_y.wait_recv()
+        relay.start()
+
+    for j in (1, 2, 3):
+        bias_wait(bias_first + z_of[j], 1, j, z_side[j])
+    bias_hop(bias_first, 4, 4, x_side)
+    gather_on(ATTN, 3)
+    gather_far(ATTN, 2)
+    bias_wait((y * 2 + 1 - x) * 4, 4, 4, x_side)
+    bias_hop(y * 8, 8, 5, y_side)
+    gather_on(UP, 0)
+    gather_far(ATTN, 3)
+    gather_on(UP, 1)
+    gather_z(DOWN)
+
+    spread_done(n1_all, 1)
+
+    @pl.when(holds_half)
+    def _():
+        relay.wait_recv()
+
+    gather_done(ATTN)
+    gather_far(UP, 0)
+
+    lane = lax.broadcasted_iota(jnp.int32, (1, 640), 1)
+    shrink = jnp.where(lane >= 384, HD ** (-0.5), 1.0).astype(f32)
+
+    def project(yy):
+        def body(tile, carry):
+            rows = rows_at(tile, 256)
+            found = dot_nn(n1_all[rows], full[ATTN, yy, :, 0:640]) + qkv_bias[yy]
+            qkv[yy, rows, 0:576] = (found * shrink)[:, 0:576].astype(bf16)
+            return carry
+
+        lax.fori_loop(0, 4, body, 0)
+
+    def attend(yy, head):
+        def body(tile, carry):
+            rows = rows_at(tile, 256)
+            keys = rows_at(tile // 2, PACK)
+            queries = qkv[yy, rows, 384 + HD * head : 448 + HD * head]
+            key_rows = qkv[yy, keys, HD * head : HD * head + HD]
+            values = qkv[yy, keys, 192 + HD * head : 256 + HD * head]
+            scores = dot_nt(queries, key_rows) + mask[rows].astype(f32)
+            exponentials = jnp.exp(scores - jnp.max(scores, axis=-1, keepdims=True))
+            totals = jnp.sum(exponentials, axis=-1, keepdims=True)
+            weights = (exponentials * (1.0 / totals)).astype(bf16)
+            probs[yy * 3 + head, rows] = weights
+            att[yy, rows, HD + HD * head : 2 * HD + HD * head] = dot_nn(weights, values).astype(bf16)
+            return carry
+
+        lax.fori_loop(0, 3, body, 0)
+
+    project(0)
+    gather_on(UP, 2)
+    project(1)
+    gather_far(UP, 1)
+    attend(0, 0)
+    gather_on(UP, 3)
+    attend(0, 1)
+    gather_far(UP, 2)
+    attend(0, 2)
+    gather_on(DOWN, 0)
+    attend(1, 0)
+    gather_far(UP, 3)
+    gather_on(DOWN, 1)
+    attend(1, 1)
+    gather_far(DOWN, 0)
+    attend(1, 2)
+    gather_on(DOWN, 2)
+
+    def out_term(rows):
+        return dot_nt(att[0, rows], full[ATTN, 0, :, 512:768]) + dot_nt(
+            att[1, rows], full[ATTN, 1, :, 512:768]
+        )
+
+    swap_sums(0, out_term)
+    gather_far(DOWN, 1)
+    bias_wait((1 - y) * 8, 8, 5, y_side)
+    for yy in (0, 1):
+        for xx in (0, 1):
+            for zz in range(4):
+                first = yy * 768 + (zz * 2 + xx) * BLK
+                bias_row[:, first : first + BLK] = bias_slots[(yy * 2 + xx) * 4 + zz, :, 0:BLK]
+    swap_done(0)
+
+    def second_norm(block, carry):
+        rows = rows_at(block, ROW)
+        values = embedded[rows] + swapped(0, rows) + biases[3:4, :]
+        hidden1[rows] = values
+        xhat, _ = row_stats(values)
+        n2_all[place(core, block)] = (xhat * gains[1:2, :] + biases[4:5, :]).astype(bf16)
+        hand_over(n2_all, 2, block).start()
+        return carry
+
+    lax.fori_loop(0, 3, second_norm, 0)
+    gather_on(DOWN, 3)
+    spread_done(n2_all, 2)
+    gather_done(UP)
+    gather_far(DOWN, 2)
+
+    def up_chunk(yy, chunk):
+        lanes = slice(chunk * 256, chunk * 256 + 256)
+        shift = bias_row[0:1, yy * 768 + chunk * 256 : yy * 768 + chunk * 256 + 256]
+
+        def body(tile, carry):
+            rows = rows_at(tile, 256)
+            before = dot_nt(n2_all[rows], full[UP, yy, lanes]) + shift
+            normal = 0.5 + 0.5 * lax.erf(before * (0.5**0.5))
+            act[yy, rows, lanes] = (before * normal).astype(bf16)
+            bell = jnp.exp(-0.5 * before * before) * ((2.0 * math.pi) ** -0.5)
+            slope[yy, rows, lanes] = (normal + before * bell).astype(bf16)
+            return carry
+
+        lax.fori_loop(0, 3, body, 0)
+
+    for yy in (0, 1):
+        for chunk in range(3):
+            up_chunk(yy, chunk)
+            if (yy, chunk) == (0, 1):
+                gather_far(DOWN, 3)
+    spread_done(g_all, 0)
+
+    def down_grad(yy):
+        for chunk in range(3):
+            lanes = slice(chunk * 256, chunk * 256 + 256)
+            part[DOWN, yy, lanes] = dot_tn(act[yy, :, lanes], g_all[...]).astype(bf16)
+
+    down_grad(1 - y)
+    gather_done(DOWN)
+    for j in (1, 2, 3, 0):
+        scatter_far(DOWN, j)
+    down_grad(y)
+
+    def du_chunk(yy, chunk):
+        lanes = slice(chunk * 256, chunk * 256 + 256)
+
+        def body(tile, carry):
+            rows = rows_at(tile, 256)
+            grad = dot_nt(g_all[rows], full[DOWN, yy, lanes]) * slope[yy, rows, lanes].astype(f32)
+            grad = grad.astype(bf16)
+            slope[yy, rows, lanes] = grad
+            return carry + column_sums(grad.astype(f32))
+
+        total = lax.fori_loop(0, 3, body, jnp.zeros((1, 256), f32))
+        for cc in (0, 1):
+            small[UP_BIAS_ROW + 2 * cc + yy : UP_BIAS_ROW + 2 * cc + yy + 1, lanes] = jnp.where(
+                core == cc, total, 0.0
+            )
+
+    def mlp_term(rows):
+        return dot_nn(act[0, rows], full[DOWN, 0]) + dot_nn(act[1, rows], full[DOWN, 1])
+
+    def du_term(rows):
+        return dot_nn(slope[0, rows], full[UP, 0]) + dot_nn(slope[1, rows], full[UP, 1])
+
+    def up_grad(yy):
+        for chunk in range(3):
+            lanes = slice(chunk * 256, chunk * 256 + 256)
+            part[UP, yy, lanes] = dot_tn(slope[yy, :, lanes], n2_all[...]).astype(bf16)
+
+    for yy in (0, 1):
+        for chunk in range(3):
+            du_chunk(yy, chunk)
+        scatter_near(DOWN, 1 + yy)
+    swap_sums(2, du_term)
+    scatter_near(DOWN, 3)
+    scatter_near(DOWN, 0)
+    up_grad(1 - y)
+    scatter_z(DOWN, 1)
+    for j in (1, 2, 3, 0):
+        scatter_far(UP, j)
+    scatter_z(DOWN, 2)
+    up_grad(y)
+    scatter_z(DOWN, 3)
+    swap_done(2)
+
+    def second_norm_back(block, carry):
+        rows = rows_at(block, ROW)
+        grad = swapped(2, rows)
+        xhat, scale = row_stats(hidden1[rows])
+        scaled = grad * gains[1:2, :]
+        back = (
+            scaled
+            - jnp.mean(scaled, axis=-1, keepdims=True)
+            - xhat * jnp.mean(scaled * xhat, axis=-1, keepdims=True)
+        ) * scale
+        given = cotangent[rows].astype(f32)
+        total = given + back
+        input_grad[rows] = total
+        dh_all[place(core, block)] = total.astype(bf16)
+        hand_over(dh_all, 3, block).start()
+        small[1:2, :] += column_sums(grad * xhat)
+        small[6:7, :] += column_sums(grad)
+        small[5:6, :] += column_sums(total)
+        small[7:8, :] += column_sums(given)
+        return carry
+
+    lax.fori_loop(0, 3, second_norm_back, 0)
+    scatter_z(DOWN, 0)
+    scatter_near(UP, 1)
+    scatter_near(UP, 2)
+    swap_sums(1, mlp_term)
+    spread_done(dh_all, 3)
+
+    def project_back(yy):
+        def body(tile, carry):
+            rows = rows_at(tile, 256)
+            datt[yy, rows] = dot_nn(dh_all[rows], full[ATTN, yy, :, 512:768]).astype(bf16)
+            return carry
+
+        lax.fori_loop(0, 3, body, 0)
+
+    def attend_back(yy, head):
+        key_acc[...] = jnp.zeros_like(key_acc)
+        value_acc[...] = jnp.zeros_like(value_acc)
+
+        def body(tile, carry):
+            rows = rows_at(tile, 256)
+            keys = rows_at(tile // 2, PACK)
+            queries = qkv[yy, rows, 384 + HD * head : 448 + HD * head]
+            key_rows = qkv[yy, keys, HD * head : HD * head + HD]
+            values = qkv[yy, keys, 192 + HD * head : 256 + HD * head]
+            grad = datt[yy, rows, HD + HD * head : 2 * HD + HD * head]
+            weights = probs[yy * 3 + head, rows]
+            weights_full = weights.astype(f32)
+            back = dot_nt(grad, values)
+            center = jnp.sum(weights_full * back, axis=-1, keepdims=True)
+            grad_scores = (weights_full * (back - center)).astype(bf16)
+            qkv[yy, rows, 384 + HD * head : 448 + HD * head] = (
+                dot_nn(grad_scores, key_rows) * HD ** (-0.5)
+            ).astype(bf16)
+            value_acc[keys] += dot_tn(weights, grad)
+            key_acc[keys] += dot_tn(grad_scores, queries)
+            return carry
+
+        lax.fori_loop(0, 3, body, 0)
+        qkv[yy, :, HD * head : HD * head + HD] = key_acc[...].astype(bf16)
+        qkv[yy, :, 192 + HD * head : 256 + HD * head] = value_acc[...].astype(bf16)
+
+    project_back(0)
+    project_back(1)
+    scatter_near(UP, 3)
+    scatter_done(DOWN)
+    attend_back(0, 0)
+    scatter_near(UP, 0)
+    attend_back(0, 1)
+    scatter_z(UP, 1)
+    attend_back(0, 2)
+    scatter_z(UP, 2)
+    attend_back(1, 0)
+    scatter_z(UP, 3)
+    attend_back(1, 1)
+    scatter_z(UP, 0)
+    attend_back(1, 2)
+
+    for yy in (0, 1):
+        start(qkv.at[yy, far_rows, 0:384], dkv_far.at[yy], far_s.at[2 + yy], far_r.at[2 + yy], y_side)
+    swap_done(1)
+
+    def finish_act(block, carry):
+        rows = rows_at(block, ROW)
+        act_out[rows] = (hidden1[rows] + swapped(1, rows) + biases[5:6, :]).astype(bf16)
+        return carry
+
+    lax.fori_loop(0, 3, finish_act, 0)
+    scatter_done(UP)
+    for yy in (0, 1):
+        copy(
+            qkv.at[yy, far_rows, 0:384], dkv_far.at[yy], far_s.at[2 + yy], far_r.at[2 + yy], y_side
+        ).wait_recv()
+        qkv[yy, half_rows, 0:384] = (
+            qkv[yy, half_rows, 0:384].astype(f32) + dkv_far[yy].astype(f32)
+        ).astype(bf16)
+
+    def attn_grad(yy):
+        for chunk in range(3):
+            lanes = slice(chunk * 256, chunk * 256 + 256)
+            n1_part = n1_all[0:CHIP, lanes]
+            part[ATTN, yy, lanes, 0:512] = dot_tn(n1_part, qkv[yy, 0:CHIP, 0:512]).astype(bf16)
+            part[ATTN, yy, lanes, 512:768] = (
+                dot_tn(n1_part, qkv[yy, 0:CHIP, 512:768]) + dot_tn(dh_all[:, lanes], att[yy])
+            ).astype(bf16)
+
+    attn_grad(1 - y)
+    for j in (1, 2, 3, 0):
+        scatter_far(ATTN, j)
+    attn_grad(y)
+
+    def in_term(rows):
+        return dot_nt(qkv[0, rows], full[ATTN, 0]) + dot_nt(qkv[1, rows], full[ATTN, 1])
+
+    scatter_near(ATTN, 1)
+    swap_sums(3, in_term)
+    scatter_near(ATTN, 2)
+    for yy in (0, 1):
+        sums = column_sums(qkv[yy, 0:CHIP, 192:576].astype(f32))
+        for cc in (0, 1):
+            first = yy * 384 + cc * 192
+            small[4:5, first : first + 192] = jnp.where(core == cc, sums[:, 0:192], 0.0)
+            small[3:4, first : first + 192] = jnp.where(core == cc, sums[:, 192:384], 0.0)
+    swap_done(3)
+    scatter_near(ATTN, 3)
+
+    def first_norm_back(block, carry):
+        rows = rows_at(block, ROW)
+        grad = swapped(3, rows)
+        xhat, scale = row_stats(embedded[rows])
+        scaled = grad * gains[0:1, :]
+        back = (
+            scaled
+            - jnp.mean(scaled, axis=-1, keepdims=True)
+            - xhat * jnp.mean(scaled * xhat, axis=-1, keepdims=True)
+        ) * scale
+        total = input_grad[rows] + back
+        input_grad[rows] = total
+        small[0:1, :] += column_sums(grad * xhat)
+        small[2:3, :] += column_sums(grad)
+        image = is_image[rows] > 0
+        small[8:9, :] += column_sums(jnp.where(image, 0.0, total))
+        small[9:10, :] += column_sums(jnp.where(image, total, 0.0))
+        return carry
+
+    lax.fori_loop(0, 3, first_norm_back, 0)
+
+    start(small, small_recv.at[4], small_s.at[4], small_r.at[4], sibling)
+    scatter_near(ATTN, 0)
+    copy(small, small_recv.at[4], small_s.at[4], small_r.at[4], sibling).wait_recv()
+    small_recv[5] = small[...] + small_recv[4]
+    start(small_recv.at[5], small_recv.at[6], small_s.at[5], small_r.at[5], x_side)
+    scatter_z(ATTN, 1)
+    copy(small_recv.at[5], small_recv.at[6], small_s.at[5], small_r.at[5], x_side).wait_recv()
+    small_recv[7] = small_recv[5] + small_recv[6]
+    start(small_recv.at[7], small_recv.at[8], small_s.at[6], small_r.at[6], y_side)
+    scatter_z(ATTN, 2)
+    copy(small_recv.at[7], small_recv.at[8], small_s.at[6], small_r.at[6], y_side).wait_recv()
+    small_recv[z] = small_recv[7] + small_recv[8]
+    for j in (1, 2, 3):
+        start(small_recv.at[z], small_recv.at[z], small_s.at[j], small_r.at[j], z_side[j])
+    scatter_z(ATTN, 3)
+    scatter_z(ATTN, 0)
+    for j in (1, 2, 3):
+        there = small_recv.at[z_of[j]]
+        copy(there, there, small_s.at[j], small_r.at[j], z_side[j]).wait_recv()
+    small_out[...] = (small_recv[0] + small_recv[1]) + (small_recv[2] + small_recv[3])
+    scatter_done(ATTN)
+
+    for one in pending:
+        one.wait_send()
+
+    @pl.when(holds_half)
+    def _():
+        over_y.wait_send()
+
+    @pl.when(jnp.logical_not(holds_half))
+    def _():
+        relay.wait_send()
+
+
+def run_layer(*operands):
+    f32, bf16 = jnp.float32, jnp.bfloat16
+    vmem, dma = pltpu.VMEM, pltpu.SemaphoreType.DMA
+    scratch = [
+        vmem((3, 2, 768, 768), bf16),
+        vmem((3, 2, 768, 768), bf16),
+        vmem((CHIP, 768), bf16),
+        vmem((CHIP + HALF_PACK, 768), bf16),
+        vmem((CHIP, 768), bf16),
+        vmem((CHIP, 768), bf16),
+        vmem((2, CHIP + HALF_PACK, 768), bf16),
+        vmem((2, CHIP, 256), bf16),
+        vmem((2, HALF_PACK, 384), bf16),
+        vmem((6, CHIP, PACK), bf16),
+        vmem((CHIP, PACK), bf16),
+        vmem((2, CHIP, 768), bf16),
+        vmem((2, CHIP, 768), bf16),
+        vmem((2, CHIP, 256), bf16),
+        vmem((CHIP + HALF_PACK, HD), f32),
+        vmem((CHIP + HALF_PACK, HD), f32),
+        vmem((OWN, 768), f32),
+        vmem((OWN, 768), f32),
+        vmem((OWN, 768), f32),
+        vmem((4, OWN, 768), bf16),
+        vmem((4, OWN, 768), bf16),
+        vmem((16, 8, 128), f32),
+        vmem((8, 1536), f32),
+        vmem((SMALL_ROWS, 768), f32),
+        vmem((9, SMALL_ROWS, 768), f32),
+        vmem((3, 4, BLK, 768), bf16),
+        vmem((3, 4, BLK, 768), bf16),
+        vmem((3, 4, HALF_BLK, 768), bf16),
+        vmem((3, 4, HALF_BLK, 768), bf16),
+        vmem((3, 4, BLK, 768), bf16),
+    ]
+    scratch += [dma((3, 4))] * 20
+    scratch += [dma((4, 3))] * 4 + [dma((4,))] * 2 + [dma((6,))] * 2 + [dma((7,))] * 2
+    whole = pl.BlockSpec(memory_space=vmem)
+    return pl.pallas_call(
+        layer_kernel,
+        out_shape=(
+            jax.ShapeDtypeStruct((OWN, 768), bf16),
+            jax.ShapeDtypeStruct((OWN, 768), f32),
+            jax.ShapeDtypeStruct((3, BLK, 768), f32),
+            jax.ShapeDtypeStruct((SMALL_ROWS, 768), f32),
+        ),
+        in_specs=[whole] * len(operands),
+        out_specs=(whole,) * 4,
+        scratch_shapes=scratch,
+        compiler_params=pltpu.CompilerParams(
+            collective_id=0, has_side_effects=True, vmem_limit_bytes=63 * 2**20
+        ),
+    )(*operands)
+
+
+def fits_kernel(mesh):
+    return dict(mesh.shape) == {"wide": 8, "narrow": 4}
+
+
+def fused_shards(
+    tokens,
+    type_ids,
+    segment_ids,
+    cotangent,
+    type_table,
+    type_first,
+    type_second,
+    norm_gains,
+    gains_first,
+    gains_second,
+    biases,
+    biases_first,
+    biases_second,
+    qkv_weight,
+    qkv_first,
+    qkv_second,
+    out_weight,
+    out_first,
+    out_second,
+    up_weight,
+    up_first,
+    up_second,
+    up_bias,
+    up_bias_first,
+    up_bias_second,
+    down_weight,
+    down_first,
+    down_second,
+):
+    f32, bf16 = jnp.float32, jnp.bfloat16
+    wide, narrow = lax.axis_index("wide"), lax.axis_index("narrow")
+    y, core = narrow // 2, narrow % 2
+    attn = jnp.concatenate(
+        [qkv_weight[1], qkv_weight[2], qkv_weight[0], out_weight.T], axis=1
+    )
+    own = jnp.stack([attn, up_weight.T, down_weight]).astype(bf16)
+    unit_bias = jnp.broadcast_to(
+        jnp.pad(up_bias.astype(bf16).astype(f32), (0, 128 - BLK))[None, :], (8, 128)
+    )
+    is_image = (type_ids == 1).astype(f32)[:, None]
+    first, middle, last = segment_ids[0], segment_ids[1], segment_ids[2]
+    early = y == 0
+    near = jnp.where(early, middle[:HALF_PACK], middle[HALF_PACK:])
+    far = jnp.where(early, middle[HALF_PACK:], middle[:HALF_PACK])
+    whole = jnp.where(early, first, last)
+    query_doc = jnp.concatenate([whole, near])[:, None]
+    key_doc = jnp.stack([whole, jnp.concatenate([near, far])])
+    by_head = biases.reshape(6, 2, 2, 192)
+    by_head = lax.dynamic_index_in_dim(by_head, core, 2, keepdims=False)
+    zeros = jnp.zeros((2, 192), f32)
+    qkv_bias = jnp.concatenate([zeros, by_head[2], by_head[1], zeros[:, :64]], axis=1)[:, None, :]
+    activations, input_grad, grads, small = run_layer(
+        own, unit_bias, tokens, is_image, cotangent, query_doc, key_doc, type_table, norm_gains,
+        biases, qkv_bias,
+    )
+    grad_attn, grad_up, grad_down = grads[0], grads[1].T, grads[2]
+    grad_qkv = jnp.stack([grad_attn[:, 384:576], grad_attn[:, 0:192], grad_attn[:, 192:384]])
+    grad_out = grad_attn[:, 576:768].T
+    grad_up_bias = lax.dynamic_slice(small, (UP_BIAS_ROW + 2 * core + y, wide * BLK), (1, BLK))[0]
+    step_sizes = step_rates()
+    updates = [
+        adam_update(type_table, type_first, type_second, small[8:10], step_sizes[0]),
+        adam_update(norm_gains, gains_first, gains_second, small[0:2], step_sizes[1]),
+        adam_update(biases, biases_first, biases_second, small[2:8], step_sizes[2]),
+        adam_update(qkv_weight, qkv_first, qkv_second, grad_qkv, step_sizes[3]),
+        adam_update(out_weight, out_first, out_second, grad_out, step_sizes[4]),
+        adam_update(up_weight, up_first, up_second, grad_up, step_sizes[5]),
+        adam_update(up_bias, up_bias_first, up_bias_second, grad_up_bias, step_sizes[6]),
+        adam_update(down_weight, down_first, down_second, grad_down, step_sizes[7]),
+    ]
+    return (activations, input_grad) + tuple(value for update in updates for value in update)
+
+
 def solution(mesh):
     placed = (
         P(("wide", "narrow"), None),
@@ -348,7 +1110,7 @@
         P(("wide", "narrow"), None),
     )
     return jax.shard_map(
-        shards,
+        fused_shards if fits_kernel(mesh) else shards,
         mesh=mesh,
         in_specs=placed,
         out_specs=(

time: 683 us -> 186 us (0.27); the launches traced: 673 us -> 186 us
  waiting for transfers between devices: 297 us -> 0 us
  Pallas kernels: 0 us -> 166 us
  blocking collectives: 149 us -> 0 us
  matrix products: 90.7 us -> 0 us
  local copies, waits for them, and re-layouts: 64.8 us -> 9.49 us
  other arithmetic: 43.8 us -> 9.35 us
  between operations: 17.1 us -> 1.1 us
  starting transfers between devices: 11 us -> 0 us
    reduce_scatter x4 -> x0, waiting for transfers between devices: 179 us -> none  [the longest x1 139 us: shards(): lax.psum_scatter(grad_down, ('wide', 'narrow'), scatter_dimension=0, tile...]
    pallas_call x0 -> x1, Pallas kernels: none -> 166 us  [run_layer(): pl.pallas_call(layer_kernel, out_shape=(jax.ShapeDtypeStruct((OWN, 768),...]
    all_gather x4 -> x0, waiting for transfers between devices: 103 us -> none  [the longest x1 58.8 us: shards(): lax.all_gather(down_low, ('wide', 'narrow'), axis=0, tiled=True)]
    dot_general x32 -> x0, matrix products: 87.4 us -> none  [the longest x3 22.3 us: times_transposed(): lax.dot_general(left_mat, right_mat, (((1,), (1,)), ((), ())), preferred_...]
    all_gather x2 -> x0, blocking collectives: 70.1 us -> none  [the longest x1 39 us: shards(): lax.all_gather(qkv_low, 'wide', axis=1, tiled=True)]
    psum x1 -> x0, blocking collectives: 40.1 us -> none  [shards(): lax.psum((gain_part, shift_part, type_part), ('wide', 'narrow'))]
    unnamed x1 -> x0, blocking collectives: 39.1 us -> none
    reduce_sum x14 -> x0, other arithmetic: 18.2 us -> none  [the longest x2 3.65 us: norm_rows(): return spread * lax.rsqrt(variance + norm_eps) * gain + shift]
  transfers between devices with their start and end apart: 10 -> 0, of which waited for: 7 -> 0; matrix products, arithmetic and copies ran while one was open for 12% -> 0% of each run, Pallas kernels for 0% -> 0%
where the time goes in v1:
time: 186 us
  Pallas kernels  166 us (89%)
  local copies, waits for them, and re-layouts  9.49 us (5%)
  other arithmetic  9.35 us (5%)
    pallas_call x1, Pallas kernels, run_layer(): pl.pallas_call(layer_kernel, out_shape=(jax.ShapeDtypeStruct((OWN, 768),...  166 us
    sub x7, other arithmetic, adam_update(): weight_in - step_rate * (direction + 0.01 * weight_in)  5.21 us
    unnamed x68, local copies, waits for them, and re-layouts  4.46 us

profile of v1, /device:TPU:0, one launch (start us, length us, event | category | flops | bytes accessed | tf_op | source)
XLA Modules:
  0.0 185.6 jit_solution(17005265655173353957)
XLA Ops:
  0.7 0.9 reshape.68
  1.7 0.1 pad.15.clone
  1.7 0.1 maximum_maximum_fusion
  1.8 0.6 broadcast_in_dim.25.qkv_bias
  2.4 0.7 broadcast_select_fusion.1
  3.1 0.8 broadcast_select_fusion
  3.9 0.9 broadcast_in_dim.27.query_doc
  4.8 0.6 pad_add_fusion.1.key_doc
  5.4 1.0 convert.29
  6.4 0.0 copy-done.13
  6.4 0.0 copy-start.25
  6.5 0.1 copy.62
  6.6 0.0 copy-start.26
  6.6 0.1 maximum_bitcast_fusion
  6.7 0.0 copy-done.2
  6.8 0.8 pad_maximum_fusion.own
  7.6 0.8 reshape.70.is_image
  8.4 0.6 broadcast_in_dim.20.unit_bias
  9.0 165.7 %shard_map.467 = (bf16[384,768]{1,0:T(8,128)(2,1)}, f32[384,768]{1,0:T(8,128)}, f32[3,96,768]{2,1,0:T(8,128)}, f32[16,768]{1,0:T(8,128)}) custom-call(bf16[3,96,768]{2,1,0:T(8,128)(2,1)} %pad_maximum_fusion.own, f32[8,128]{1,0:T(8,128)} %broadcast_in_dim.20.unit_bias, bf16[384,768]{1,0:T(8,128)(2,1)} %tokens.1, f32[384,1]{1,0:T(8,128)} %reshape.70.is_image, ...), custom_call_target="tpu_custom_call" | custom-call | tf_op jit(solution)/shard_map/pallas_call | solution.py:986
  174.7 0.0 copy-start.6
  174.7 0.0 copy-start.7
  174.7 1.0 slice_bitcast_fusion
  175.8 0.1 slice_bitcast_fusion.4
  175.9 0.0 copy-start.14
  175.9 0.0 copy-start.15
  175.9 1.1 multiply_subtract_fusion.2
  177.0 0.1 copy.66
  177.1 0.1 copy.67
  177.2 0.2 multiply_subtract_fusion.3
  177.3 0.7 copy.70
  178.1 0.7 copy.71
  178.8 0.7 copy.72
  179.6 1.1 multiply_subtract_fusion.1
  180.6 0.0 copy-start.12
  180.6 0.0 copy-start.17
  180.7 0.0 copy-start.18
  180.7 0.0 copy-start.19
  180.7 0.0 copy-start.20
  180.7 0.0 copy-start.21
  180.7 0.0 copy-start.22
  180.7 0.0 copy-start.23
  180.7 0.0 copy-start.24
  180.8 1.1 multiply_subtract_fusion
  181.8 0.6 multiply_subtract_fusion.7
  182.5 0.6 multiply_subtract_fusion.4
  183.1 0.6 multiply_subtract_fusion.5
  183.8 0.8 copy.80
  184.6 1.0 copy.81
  (57 shorter events, 0.2 us)
Async XLA Ops:
  0.7 5.8 %copy-start.13 = (f32[192,96]{1,0:T(8,128)S(1)}, f32[192,96]{1,0:T(8,128)}, u32[]{:S(2)}) copy-start(f32[192,96]{1,0:T(8,128)} %param.44) | copy-start | bytes 221188
  0.7 6.0 %copy-start.3 = (f32[96,768]{1,0:T(8,128)S(1)}, f32[96,768]{1,0:T(8,128)}, u32[]{:S(2)}) copy-start(f32[96,768]{1,0:T(8,128)} %param.53) | copy-start | bytes 884740
  1.7 5.0 %copy-start.2 = (f32[768,96]{0,1:T(8,128)S(1)}, f32[768,96]{0,1:T(8,128)}, u32[]{:S(2)}) copy-start(f32[768,96]{0,1:T(8,128)} %param.47) | copy-start | bytes 884740
  6.4 1.1 copy-start.25
  6.6 1.8 copy-start.26
  9.0 166.9 %copy-start.1 = (f32[3,96,192]{2,1,0:T(8,128)S(1)}, f32[3,96,192]{2,1,0:T(8,128)}, u32[]{:S(2)}) copy-start(f32[3,96,192]{2,1,0:T(8,128)} %param.41) | copy-start | bytes 663556
  174.7 1.2 copy-start.6
  174.7 1.2 copy-start.7
  175.9 1.1 copy-start.14
  175.9 1.2 copy-start.15
  177.0 2.6 %copy-start.4 = (f32[3,96,768]{2,1,0:T(8,128)S(1)}, f32[3,96,768]{2,1,0:T(8,128)}, u32[]{:S(2)}) copy-start(f32[3,96,768]{2,1,0:T(8,128)} %get-tuple-element.33) | copy-start | bytes 2654212
  177.0 2.6 %copy-start.8 = (f32[768,96]{0,1:T(8,128)S(1)}, f32[768,96]{0,1:T(8,128)}, u32[]{:S(2)}) copy-start(f32[768,96]{0,1:T(8,128)} %param.48) | copy-start | bytes 884740
  177.0 2.6 %copy-start.9 = (f32[768,96]{0,1:T(8,128)S(1)}, f32[768,96]{0,1:T(8,128)}, u32[]{:S(2)}) copy-start(f32[768,96]{0,1:T(8,128)} %param.49) | copy-start | bytes 884740
  178.8 1.9 %copy-start.10 = (f32[96,768]{1,0:T(8,128)S(1)}, f32[96,768]{1,0:T(8,128)}, u32[]{:S(2)}) copy-start(f32[96,768]{1,0:T(8,128)} %param.54) | copy-start | bytes 884740
  178.8 1.9 %copy-start.11 = (f32[96,768]{1,0:T(8,128)S(1)}, f32[96,768]{1,0:T(8,128)}, u32[]{:S(2)}) copy-start(f32[96,768]{1,0:T(8,128)} %param.55) | copy-start | bytes 884740
  180.6 1.2 copy-start.16
  180.6 1.2 copy-start.27
  180.6 1.2 copy-start.28
  180.6 1.2 copy-start.29
  180.6 1.8 copy-start.12
  180.6 1.8 copy-start.17
  180.7 1.8 copy-start.18
  180.7 2.4 %copy-start.19 = (f32[2,768]{1,0:T(2,128)S(1)}, f32[2,768]{1,0:T(2,128)}, u32[]{:S(2)}) copy-start(f32[2,768]{1,0:T(2,128)} %type_table.1) | copy-start | bytes 18436
  180.7 2.4 %copy-start.20 = (f32[2,768]{1,0:T(2,128)S(1)}, f32[2,768]{1,0:T(2,128)}, u32[]{:S(2)}) copy-start(f32[2,768]{1,0:T(2,128)} %gains.1) | copy-start | bytes 18436
  180.7 2.4 %copy-start.21 = (f32[2,768]{1,0:T(2,128)S(1)}, f32[2,768]{1,0:T(2,128)}, u32[]{:S(2)}) copy-start(f32[2,768]{1,0:T(2,128)} %param.36) | copy-start | bytes 18436
  180.7 2.4 %copy-start.22 = (f32[2,768]{1,0:T(2,128)S(1)}, f32[2,768]{1,0:T(2,128)}, u32[]{:S(2)}) copy-start(f32[2,768]{1,0:T(2,128)} %param.37) | copy-start | bytes 18436
  180.7 2.4 %copy-start.23 = (f32[2,768]{1,0:T(2,128)S(1)}, f32[2,768]{1,0:T(2,128)}, u32[]{:S(2)}) copy-start(f32[2,768]{1,0:T(2,128)} %param.34) | copy-start | bytes 18436
  180.7 2.4 %copy-start.24 = (f32[2,768]{1,0:T(2,128)S(1)}, f32[2,768]{1,0:T(2,128)}, u32[]{:S(2)}) copy-start(f32[2,768]{1,0:T(2,128)} %param.33) | copy-start | bytes 18436
  180.8 3.0 %copy-start.5 = (bf16[384,768]{1,0:T(8,128)(2,1)S(1)}, bf16[384,768]{1,0:T(8,128)(2,1)}, u32[]{:S(2)}) copy-start(bf16[384,768]{1,0:T(8,128)(2,1)} %get-tuple-element.151) | copy-start | bytes 1769476
  181.8 2.8 %copy-start = (f32[384,768]{1,0:T(8,128)S(1)}, f32[384,768]{1,0:T(8,128)}, u32[]{:S(2)}) copy-start(f32[384,768]{1,0:T(8,128)} %get-tuple-element.152) | copy-start | bytes 3538948

commit v2 on v0

--- a/solution.py
+++ b/solution.py
@@ -1,6 +1,10 @@
+import math
+
 import jax
 import jax.numpy as jnp
 from jax import lax
+from jax.experimental import pallas as pl
+from jax.experimental.pallas import tpu as pltpu
 from jax.sharding import PartitionSpec as P
 
 D = 768
@@ -316,6 +320,1056 @@
     )
 
 
+def dot_nn(left_mat, right_mat):
+    return lax.dot_general(
+        left_mat, right_mat, (((1,), (0,)), ((), ())), preferred_element_type=jnp.float32
+    )
+
+
+def dot_nt(left_mat, right_mat):
+    return lax.dot_general(
+        left_mat, right_mat, (((1,), (1,)), ((), ())), preferred_element_type=jnp.float32
+    )
+
+
+def dot_tn(left_mat, right_mat):
+    return lax.dot_general(
+        left_mat, right_mat, (((0,), (0,)), ((), ())), preferred_element_type=jnp.float32
+    )
+
+
+def rows_at(block, size):
+    return pl.ds(pl.multiple_of(block * size, size), size)
+
+
+def row_stats(values):
+    center = jnp.mean(values, axis=-1, keepdims=True)
+    spread = values - center
+    variance = jnp.mean(spread * spread, axis=-1, keepdims=True)
+    scale = lax.rsqrt(variance + norm_eps)
+    return spread * scale, scale
+
+
+def column_sums(values):
+    return jnp.sum(values, axis=0, keepdims=True)
+
+
+ROW = 128
+OWN = 384
+CHIP = 768
+HALF_PACK = 256
+PACK = 512
+BLK = 96
+ATTN, UP, DOWN = 0, 1, 2
+Z_FIRST = (96, 64, 64)
+Z_LAST = 32
+LAST_AT = 512
+GATHER_BY_Y = (32, 32, 32)
+SCATTER_BY_Y = (48, 16, 16)
+GAIN_ROW, BIAS_ROW, TYPE_ROW, UP_BIAS_ROW, SMALL_ROWS = 0, 2, 8, 10, 16
+
+
+def layer_kernel(
+    qkv_weight, out_weight, up_rows, down_rows, up_bias, tokens, type_ids, cotangent, segment_ids, type_table,
+    gains, biases,
+    act_out, input_grad, qkv_grad, out_grad, up_out, down_out, small_out,
+    full, part, g_all, n1_all, n2_all, dh_all, qkv, att, dkv_far, probs, mask, act, slope, datt,
+    key_acc, value_acc, embedded, hidden1, own_sum, attn_out, swap_send, swap_recv, type_cols, qkv_bias,
+    bias_slots, bias_row, small, small_recv, rx, ry, rdx, rdy, rz, rl,
+    gz_s, gz_r, gx_s, gx_r, gy_s, gy_r, gfx_s, gfx_r, gfy_s, gfy_r,
+    sz_s, sz_r, sx_s, sx_r, sy_s, sy_r, sdx_s, sdx_r, sdy_s, sdy_r,
+    gl_s, gl_r, sl_s, sl_r, glz_s, glz_r, slz_s, slz_r,
+    spread_s, spread_r, swap_s, swap_r, far_s, far_r, bias_s, bias_r, small_s, small_r,
+):
+    f32, bf16 = jnp.float32, jnp.bfloat16
+    wide = lax.axis_index("wide")
+    narrow = lax.axis_index("narrow")
+    z, x = wide // 2, wide % 2
+    y, core = narrow // 2, narrow % 2
+    z_of = [z, z + 1 - 2 * (z % 2), (z + 2) % 4, 3 - z]
+    sibling = (wide, y * 2 + (1 - core))
+    x_side = (z * 2 + (1 - x), narrow)
+    y_side = (wide, (1 - y) * 2 + core)
+    z_side = [None] + [(z_of[j] * 2 + x, narrow) for j in (1, 2, 3)]
+
+    def copy(src, dst, send, recv, to):
+        return pltpu.make_async_remote_copy(
+            src_ref=src, dst_ref=dst, send_sem=send, recv_sem=recv, device_id=to,
+            device_id_type=pl.DeviceIdType.MESH,
+        )
+
+    pending = []
+    pending_if = []
+    totals = (attn_out, up_out, down_out)
+
+    def start(*args):
+        one = copy(*args)
+        one.start()
+        pending.append(one)
+        return one
+
+    barrier = pltpu.get_barrier_semaphore()
+    for to in (sibling, x_side, y_side, z_side[1], z_side[2], z_side[3]):
+        pl.semaphore_signal(barrier, inc=1, device_id=to, device_id_type=pl.DeviceIdType.MESH)
+    pl.semaphore_wait(barrier, 6)
+
+    inner = z * (3 - z) == 2
+    outer = z * (3 - z) == 0
+
+    def start_if(which, *args):
+        one = copy(*args)
+
+        @pl.when(which)
+        def _():
+            one.start()
+
+        pending_if.append((which, one))
+
+    def slot(ref, kind, yy, zz, xx, first=0, size=None):
+        rows = Z_FIRST[kind]
+        row = pl.multiple_of((zz * 2 + xx) * rows + first, 16)
+        return ref.at[kind, yy, pl.ds(row, rows if size is None else size)]
+
+    def last(ref, kind, yy, zz, xx, first=0, size=Z_LAST):
+        row = pl.multiple_of(LAST_AT + (zz * 2 + xx) * Z_LAST + first, 16)
+        return ref.at[kind, yy, pl.ds(row, size)]
+
+    def last_pair(ref, kind, yy, zz):
+        return last(ref, kind, yy, zz, 0, 0, 2 * Z_LAST)
+
+    def gather_z(kind):
+        mine = slot(full, kind, y, z, x)
+        for j in (1, 2):
+            start(mine, mine, gz_s.at[kind, j], gz_r.at[kind, j], z_side[j])
+        start_if(inner, mine, mine, gz_s.at[kind, 3], gz_r.at[kind, 3], z_side[3])
+
+    def gather_on(kind, j):
+        block = slot(full, kind, y, z_of[j], x)
+        if j:
+            copy(block, block, gz_s.at[kind, j], gz_r.at[kind, j], z_side[j]).wait_recv()
+        if j == 2:
+            start_if(inner, block, block, gz_s.at[kind, 0], gz_r.at[kind, 3], z_side[1])
+        start(block, block, gx_s.at[kind, j], gx_r.at[kind, j], x_side)
+        start(block, block, gy_s.at[kind, j], gy_r.at[kind, j], y_side)
+        if kind != ATTN and j == 0:
+            block = last(full, kind, y, z, x)
+            start(block, block, gl_s.at[kind, 0], gl_r.at[kind, 0], x_side)
+            start(block, block, gl_s.at[kind, 1], gl_r.at[kind, 1], y_side)
+
+    def gather_far(kind, j):
+        zz = z_of[j]
+        by_y, by_x = GATHER_BY_Y[kind], Z_FIRST[kind] - GATHER_BY_Y[kind]
+        block = slot(full, kind, y, zz, 1 - x)
+        copy(block, block, gx_s.at[kind, j], gx_r.at[kind, j], x_side).wait_recv()
+        half = slot(full, kind, y, zz, 1 - x, 0, by_y)
+        start(half, half, gfy_s.at[kind, j], gfy_r.at[kind, j], y_side)
+        block = slot(full, kind, 1 - y, zz, x)
+        copy(block, block, gy_s.at[kind, j], gy_r.at[kind, j], y_side).wait_recv()
+        half = slot(full, kind, 1 - y, zz, x, by_y, by_x)
+        start(half, half, gfx_s.at[kind, j], gfx_r.at[kind, j], x_side)
+        if kind != ATTN and j == 0:
+            block = last(full, kind, y, z, 1 - x)
+            copy(block, block, gl_s.at[kind, 0], gl_r.at[kind, 0], x_side).wait_recv()
+            half = last(full, kind, y, z, 1 - x, 0, 16)
+            start(half, half, gl_s.at[kind, 2], gl_r.at[kind, 2], y_side)
+            block = last(full, kind, 1 - y, z, x)
+            copy(block, block, gl_s.at[kind, 1], gl_r.at[kind, 1], y_side).wait_recv()
+            half = last(full, kind, 1 - y, z, x, 16, 16)
+            start(half, half, gl_s.at[kind, 3], gl_r.at[kind, 3], x_side)
+
+    def gather_last(kind):
+        half = last(full, kind, 1 - y, z, 1 - x, 0, 16)
+        copy(half, half, gl_s.at[kind, 2], gl_r.at[kind, 2], y_side).wait_recv()
+        half = last(full, kind, 1 - y, z, 1 - x, 16, 16)
+        copy(half, half, gl_s.at[kind, 3], gl_r.at[kind, 3], x_side).wait_recv()
+        for yy in (0, 1):
+            pair = last_pair(full, kind, yy, z)
+            for j in (1, 2):
+                start(pair, pair, glz_s.at[kind, 2 * j + yy], glz_r.at[kind, 2 * j + yy], z_side[j])
+            start_if(inner, pair, pair, glz_s.at[kind, 6 + yy], glz_r.at[kind, 6 + yy], z_side[3])
+
+    def last_arrived(kind, j):
+        for yy in (0, 1):
+            pair = last_pair(full, kind, yy, z_of[j])
+            copy(pair, pair, glz_s.at[kind, 2 * j + yy], glz_r.at[kind, 2 * j + yy], z_side[j]).wait_recv()
+
+    def gather_relay(kind):
+        last_arrived(kind, 2)
+        for yy in (0, 1):
+            pair = last_pair(full, kind, yy, z_of[2])
+            start_if(inner, pair, pair, glz_s.at[kind, yy], glz_r.at[kind, 6 + yy], z_side[1])
+
+    def gather_last_done(kind):
+        last_arrived(kind, 1)
+        last_arrived(kind, 3)
+
+    def gather_done(kind):
+        by_y, by_x = GATHER_BY_Y[kind], Z_FIRST[kind] - GATHER_BY_Y[kind]
+        for j in range(4):
+            half = slot(full, kind, 1 - y, z_of[j], 1 - x, 0, by_y)
+            copy(half, half, gfy_s.at[kind, j], gfy_r.at[kind, j], y_side).wait_recv()
+            half = slot(full, kind, 1 - y, z_of[j], 1 - x, by_y, by_x)
+            copy(half, half, gfx_s.at[kind, j], gfx_r.at[kind, j], x_side).wait_recv()
+
+    def add_in(ref, arrived):
+        ref[...] = (ref[...].astype(f32) + arrived[...].astype(f32)).astype(bf16)
+
+    def scatter_last(kind):
+        for yy in (0, 1):
+            def target(j):
+                return last_pair(part, kind, yy, z_of[j])
+
+            def landing(j):
+                return rl.at[kind - 1, j, yy]
+
+            def sems(sent, landed):
+                return slz_s.at[kind, 2 * sent + yy], slz_r.at[kind, 2 * landed + yy]
+
+            start(target(1), landing(1), *sems(1, 1), z_side[1])
+            start_if(outer, target(2), landing(2), *sems(2, 2), z_side[2])
+            start_if(inner, target(3), landing(3), *sems(3, 3), z_side[3])
+            start_if(outer, target(3), landing(0), *sems(3, 0), z_side[1])
+
+    def scatter_relay(kind):
+        @pl.when(inner)
+        def _():
+            for yy in (0, 1):
+                here = last_pair(part, kind, yy, z_of[2])
+                came = rl.at[kind - 1, 0, yy]
+                copy(here, came, slz_s.at[kind, yy], slz_r.at[kind, yy], z_side[1]).wait_recv()
+                add_in(here, came)
+
+        for yy in (0, 1):
+            here = last_pair(part, kind, yy, z_of[2])
+            start_if(
+                inner, here, rl.at[kind - 1, 2, yy], slz_s.at[kind, 4 + yy], slz_r.at[kind, 4 + yy], z_side[2]
+            )
+
+    def scatter_last_add(kind):
+        for yy in (0, 1):
+            here = last_pair(part, kind, yy, z)
+            for j in (1, 2):
+                came = rl.at[kind - 1, j, yy]
+                copy(here, came, slz_s.at[kind, 2 * j + yy], slz_r.at[kind, 2 * j + yy], z_side[j]).wait_recv()
+            total = here[...].astype(f32) + rl[kind - 1, 1, yy].astype(f32) + rl[kind - 1, 2, yy].astype(f32)
+            here[...] = total.astype(bf16)
+
+        @pl.when(inner)
+        def _():
+            for yy in (0, 1):
+                here = last_pair(part, kind, yy, z)
+                came = rl.at[kind - 1, 3, yy]
+                copy(here, came, slz_s.at[kind, 6 + yy], slz_r.at[kind, 6 + yy], z_side[3]).wait_recv()
+                add_in(here, came)
+
+    def scatter_far(kind, j):
+        by_y, by_x = SCATTER_BY_Y[kind], Z_FIRST[kind] - SCATTER_BY_Y[kind]
+        half = slot(part, kind, 1 - y, z_of[j], 1 - x, 0, by_y)
+        start(half, rdy.at[kind, j, pl.ds(0, by_y)], sdy_s.at[kind, j], sdy_r.at[kind, j], y_side)
+        half = slot(part, kind, 1 - y, z_of[j], 1 - x, by_y, by_x)
+        start(half, rdx.at[kind, j, pl.ds(0, by_x)], sdx_s.at[kind, j], sdx_r.at[kind, j], x_side)
+        if kind != ATTN and j == 0:
+            half = last(part, kind, 1 - y, z, 1 - x, 0, 16)
+            start(half, rdy.at[kind, 0, pl.ds(48, 16)], sl_s.at[kind, 0], sl_r.at[kind, 0], y_side)
+            half = last(part, kind, 1 - y, z, 1 - x, 16, 16)
+            start(half, rdx.at[kind, 0, pl.ds(48, 16)], sl_s.at[kind, 1], sl_r.at[kind, 1], x_side)
+
+    def scatter_near(kind, j):
+        zz = z_of[j]
+        rows = Z_FIRST[kind]
+        by_y, by_x = SCATTER_BY_Y[kind], rows - SCATTER_BY_Y[kind]
+        half = slot(part, kind, y, zz, 1 - x, 0, by_y)
+        came = rdy.at[kind, j, pl.ds(0, by_y)]
+        copy(half, came, sdy_s.at[kind, j], sdy_r.at[kind, j], y_side).wait_recv()
+        add_in(half, came)
+        land = pl.ds(0, rows)
+        start(slot(part, kind, y, zz, 1 - x), rx.at[kind, j, land], sx_s.at[kind, j], sx_r.at[kind, j], x_side)
+        half = slot(part, kind, 1 - y, zz, x, by_y, by_x)
+        came = rdx.at[kind, j, pl.ds(0, by_x)]
+        copy(half, came, sdx_s.at[kind, j], sdx_r.at[kind, j], x_side).wait_recv()
+        add_in(half, came)
+        start(slot(part, kind, 1 - y, zz, x), ry.at[kind, j, land], sy_s.at[kind, j], sy_r.at[kind, j], y_side)
+        if kind != ATTN and j == 0:
+            land = pl.ds(rows, Z_LAST)
+            half = last(part, kind, y, z, 1 - x, 0, 16)
+            came = rdy.at[kind, 0, pl.ds(48, 16)]
+            copy(half, came, sl_s.at[kind, 0], sl_r.at[kind, 0], y_side).wait_recv()
+            add_in(half, came)
+            start(last(part, kind, y, z, 1 - x), rx.at[kind, 0, land], sl_s.at[kind, 2], sl_r.at[kind, 2], x_side)
+            half = last(part, kind, 1 - y, z, x, 16, 16)
+            came = rdx.at[kind, 0, pl.ds(48, 16)]
+            copy(half, came, sl_s.at[kind, 1], sl_r.at[kind, 1], x_side).wait_recv()
+            add_in(half, came)
+            start(last(part, kind, 1 - y, z, x), ry.at[kind, 0, land], sl_s.at[kind, 3], sl_r.at[kind, 3], y_side)
+
+    def scatter_z(kind, j):
+        land = pl.ds(0, Z_FIRST[kind])
+        block = slot(part, kind, y, z_of[j], x)
+        copy(block, rx.at[kind, j, land], sx_s.at[kind, j], sx_r.at[kind, j], x_side).wait_recv()
+        copy(block, ry.at[kind, j, land], sy_s.at[kind, j], sy_r.at[kind, j], y_side).wait_recv()
+        total = block[...].astype(f32) + rx[kind, j, land].astype(f32) + ry[kind, j, land].astype(f32)
+        if j == 0:
+            totals[kind][land] = total
+            if kind != ATTN:
+                land = pl.ds(Z_FIRST[kind], Z_LAST)
+                block = last(part, kind, y, z, x)
+                copy(block, rx.at[kind, 0, land], sl_s.at[kind, 2], sl_r.at[kind, 2], x_side).wait_recv()
+                copy(block, ry.at[kind, 0, land], sl_s.at[kind, 3], sl_r.at[kind, 3], y_side).wait_recv()
+                totals[kind][land] = (
+                    block[...].astype(f32) + rx[kind, 0, land].astype(f32) + ry[kind, 0, land].astype(f32)
+                )
+            return
+        block[...] = total.astype(bf16)
+        came = rz.at[kind, j, land]
+        if j == 1:
+            start(block, came, sz_s.at[kind, j], sz_r.at[kind, j], z_side[j])
+        elif j == 2:
+            relayed = rz.at[kind, 0, land]
+
+            @pl.when(inner)
+            def _():
+                copy(block, relayed, sz_s.at[kind, 0], sz_r.at[kind, 0], z_side[1]).wait_recv()
+                add_in(block, relayed)
+
+            start(block, came, sz_s.at[kind, j], sz_r.at[kind, j], z_side[j])
+        else:
+            start_if(inner, block, came, sz_s.at[kind, 3], sz_r.at[kind, 3], z_side[3])
+            start_if(outer, block, rz.at[kind, 0, land], sz_s.at[kind, 3], sz_r.at[kind, 0], z_side[1])
+
+    def scatter_done(kind):
+        land = pl.ds(0, Z_FIRST[kind])
+        for j in (1, 2):
+            came = rz.at[kind, j, land]
+            copy(came, came, sz_s.at[kind, j], sz_r.at[kind, j], z_side[j]).wait_recv()
+        totals[kind][land] += rz[kind, 1, land].astype(f32) + rz[kind, 2, land].astype(f32)
+
+        @pl.when(inner)
+        def _():
+            came = rz.at[kind, 3, land]
+            copy(came, came, sz_s.at[kind, 3], sz_r.at[kind, 3], z_side[3]).wait_recv()
+            totals[kind][land] += came[...].astype(f32)
+
+    def place(which, block):
+        return rows_at((3 * which + block + 4 * y) % 6, ROW)
+
+    def hand_over(ref, use, block):
+        here = ref.at[place(core, block)]
+        return copy(here, here, spread_s.at[use, block], spread_r.at[use, block], sibling)
+
+    def spread_done(ref, use):
+        for block in range(3):
+            there = ref.at[place(1 - core, block)]
+            copy(there, there, spread_s.at[use, block], spread_r.at[use, block], sibling).wait_recv()
+            pending.append(hand_over(ref, use, block))
+
+    def swap_sums(use, term):
+        def for_sibling(block, carry):
+            rows = rows_at(block, ROW)
+            swap_send[rows] = term(place(1 - core, block)).astype(bf16)
+            copy(
+                swap_send.at[rows], swap_recv.at[use, rows], swap_s.at[use, block],
+                swap_r.at[use, block], sibling,
+            ).start()
+            return carry
+
+        def for_self(block, carry):
+            own_sum[rows_at(block, ROW)] = term(place(core, block))
+            return carry
+
+        lax.fori_loop(0, 3, for_sibling, 0)
+        lax.fori_loop(0, 3, for_self, 0)
+
+    def swap_done(use):
+        for block in range(3):
+            rows = pl.ds(block * ROW, ROW)
+            one = copy(
+                swap_send.at[rows], swap_recv.at[use, rows], swap_s.at[use, block],
+                swap_r.at[use, block], sibling,
+            )
+            one.wait_recv()
+            one.wait_send()
+
+    def swapped(use, rows):
+        return own_sum[rows] + swap_recv[use, rows].astype(f32)
+
+    def own_attn():
+        slot(full, ATTN, y, z, x)[...] = jnp.concatenate(
+            [qkv_weight[1], qkv_weight[2], qkv_weight[0], out_weight[...].T], axis=1
+        ).astype(bf16)
+
+    def own_rest():
+        for kind, rows in ((UP, up_rows), (DOWN, down_rows)):
+            slot(full, kind, y, z, x)[...] = rows[0:64].astype(bf16)
+            last(full, kind, y, z, x)[...] = rows[64:96].astype(bf16)
+
+    def as_column(row):
+        return jnp.broadcast_to(row, (ROW, ROW)).T
+
+    def column_types():
+        types = type_ids[...].astype(f32)
+        for block in range(3):
+            rows = pl.ds(block * ROW, ROW)
+            type_cols[rows] = as_column(types[:, block * ROW : block * ROW + ROW])
+
+    def give_cotangent():
+        def body(block, carry):
+            g_all[place(core, block)] = cotangent[rows_at(block, ROW)]
+            hand_over(g_all, 0, block).start()
+            return carry
+
+        lax.fori_loop(0, 3, body, 0)
+
+    def first_norm():
+        def body(block, carry):
+            rows = rows_at(block, ROW)
+            values = tokens[rows].astype(f32) + jnp.where(
+                type_cols[rows, 0:1] > 0, type_table[1:2, :], type_table[0:1, :]
+            )
+            embedded[rows] = values
+            xhat, _ = row_stats(values)
+            n1_all[place(core, block)] = (xhat * gains[0:1, :] + biases[0:1, :]).astype(bf16)
+            hand_over(n1_all, 1, block).start()
+            return carry
+
+        lax.fori_loop(0, 3, body, 0)
+
+    half_rows = pl.ds(PACK, HALF_PACK)
+    far_rows = pl.ds(CHIP, HALF_PACK)
+    over_y = copy(n1_all.at[half_rows], n1_all.at[far_rows], far_s.at[0], far_r.at[0], y_side)
+    relay = copy(n1_all.at[far_rows], n1_all.at[far_rows], far_s.at[1], far_r.at[1], sibling)
+    holds_half = (core + y) == 1
+
+    def half_over():
+        @pl.when(holds_half)
+        def _():
+            over_y.start()
+
+    def half_relay():
+        @pl.when(jnp.logical_not(holds_half))
+        def _():
+            over_y.wait_recv()
+            relay.start()
+
+    def half_arrived():
+        @pl.when(holds_half)
+        def _():
+            relay.wait_recv()
+
+    bias_first = (y * 2 + x) * 4
+
+    def bias_hop(first, size, index, to):
+        ref = bias_slots.at[pl.ds(first, size)]
+        return start(ref, ref, bias_s.at[index], bias_r.at[index], to)
+
+    def bias_wait(first, size, index, to):
+        ref = bias_slots.at[pl.ds(first, size)]
+        copy(ref, ref, bias_s.at[index], bias_r.at[index], to).wait_recv()
+
+    def bias_along_z():
+        bias_slots[bias_first + z] = jnp.broadcast_to(
+            jnp.concatenate(
+                [up_bias[...].astype(bf16).astype(f32), jnp.zeros((1, 128 - BLK), f32)], axis=1
+            ),
+            (8, 128),
+        )
+        for j in (1, 2, 3):
+            bias_hop(bias_first + z, 1, j, z_side[j])
+
+    def bias_along_x():
+        for j in (1, 2, 3):
+            bias_wait(bias_first + z_of[j], 1, j, z_side[j])
+        bias_hop(bias_first, 4, 4, x_side)
+
+    def bias_along_y():
+        bias_wait((y * 2 + 1 - x) * 4, 4, 4, x_side)
+        bias_hop(y * 8, 8, 5, y_side)
+
+    def bias_as_rows():
+        bias_wait((1 - y) * 8, 8, 5, y_side)
+        for yy in (0, 1):
+            for xx in (0, 1):
+                for zz in range(4):
+                    which, block = zz * 2 + xx, (yy * 2 + xx) * 4 + zz
+                    bias_row[yy, :, which * 64 : which * 64 + 64] = bias_slots[block, :, 0:64]
+                    first = LAST_AT + which * Z_LAST
+                    bias_row[yy, :, first : first + Z_LAST] = bias_slots[block, :, 64:96]
+
+    def masks():
+        documents = segment_ids[...].astype(f32)
+        early = y == 0
+        whole_doc = jnp.where(early, documents[0:1], documents[2:3])
+        near_doc = jnp.where(early, documents[1:2, 0:256], documents[1:2, 256:512])
+        far_doc = jnp.where(early, documents[1:2, 256:512], documents[1:2, 0:256])
+        query_rows = (whole_doc[:, 0:256], whole_doc[:, 256:512], near_doc)
+        key_rows_of = (whole_doc, jnp.concatenate([near_doc, far_doc], axis=1))
+        for side, tiles in ((0, (0, 1)), (1, (2,))):
+            for chunk in range(4):
+                keys = slice(chunk * ROW, chunk * ROW + ROW)
+                column = as_column(key_rows_of[side][:, keys])[:, 0:1]
+                for tile in tiles:
+                    mask[tile, keys] = jnp.where(
+                        column == query_rows[tile], 0.0, masked_score
+                    ).astype(bf16)
+
+    def zeros_and_biases():
+        small[...] = jnp.zeros_like(small)
+        for yy in (0, 1):
+            att[yy, :, 0:HD] = jnp.zeros((CHIP, HD), bf16)
+            qkv[yy, :, 576:768] = jnp.zeros((CHIP + HALF_PACK, 192), bf16)
+            first = yy * 384
+            chosen = [
+                jnp.where(
+                    core == 0,
+                    biases[i : i + 1, first : first + 192],
+                    biases[i : i + 1, first + 192 : first + 384],
+                )
+                for i in (2, 1)
+            ]
+            zeros = jnp.zeros((1, 192), f32)
+            qkv_bias[yy] = jnp.concatenate([zeros] + chosen + [zeros[:, 0:64]], axis=1)
+
+    lane = lax.broadcasted_iota(jnp.int32, (1, 640), 1)
+    shrink = jnp.where(lane >= 384, HD ** (-0.5), 1.0).astype(f32)
+
+    def project(yy):
+        def body(tile, carry):
+            rows = rows_at(tile, 256)
+            found = dot_nn(n1_all[rows], full[ATTN, yy, :, 0:640]) + qkv_bias[yy]
+            qkv[yy, rows, 0:576] = (found * shrink)[:, 0:576].astype(bf16)
+            return carry
+
+        lax.fori_loop(0, 4, body, 0)
+
+    def head_rows(yy, head, rows, keys):
+        queries = qkv[yy, rows, 384 + HD * head : 448 + HD * head]
+        key_rows = qkv[yy, keys, HD * head : HD * head + HD]
+        values = qkv[yy, keys, 192 + HD * head : 256 + HD * head]
+        return queries, key_rows, values
+
+    def attend(yy, head):
+        def body(tile, carry):
+            rows = rows_at(tile, 256)
+            queries, key_rows, values = head_rows(yy, head, rows, rows_at(tile // 2, PACK))
+            scores = dot_nt(key_rows, queries) + mask[tile].astype(f32)
+            exponentials = jnp.exp(scores - jnp.max(scores, axis=0, keepdims=True))
+            totals = jnp.sum(exponentials, axis=0, keepdims=True)
+            weights = (exponentials * (1.0 / totals)).astype(bf16)
+            probs[yy * 3 + head, tile] = weights
+            att[yy, rows, HD + HD * head : 2 * HD + HD * head] = dot_tn(values, weights).T.astype(bf16)
+            return carry
+
+        lax.fori_loop(0, 3, body, 0)
+
+    def out_term(rows):
+        return dot_nt(att[0, rows], full[ATTN, 0, :, 512:768]) + dot_nt(
+            att[1, rows], full[ATTN, 1, :, 512:768]
+        )
+
+    def second_norm():
+        def body(block, carry):
+            rows = rows_at(block, ROW)
+            values = embedded[rows] + swapped(0, rows) + biases[3:4, :]
+            hidden1[rows] = values
+            xhat, _ = row_stats(values)
+            n2_all[place(core, block)] = (xhat * gains[1:2, :] + biases[4:5, :]).astype(bf16)
+            hand_over(n2_all, 2, block).start()
+            return carry
+
+        lax.fori_loop(0, 3, body, 0)
+
+    def up_chunk(yy, chunk):
+        lanes = slice(chunk * 256, chunk * 256 + 256)
+        shift = bias_row[yy, 0:1, lanes]
+
+        def body(tile, carry):
+            rows = rows_at(tile, 256)
+            before = dot_nt(n2_all[rows], full[UP, yy, lanes]) + shift
+            normal = 0.5 + 0.5 * lax.erf(before * (0.5**0.5))
+            act[yy, rows, lanes] = (before * normal).astype(bf16)
+            bell = jnp.exp(-0.5 * before * before) * ((2.0 * math.pi) ** -0.5)
+            slope[yy, rows, lanes] = (normal + before * bell).astype(bf16)
+            return carry
+
+        lax.fori_loop(0, 3, body, 0)
+
+    def down_grad(yy):
+        for chunk in range(3):
+            lanes = slice(chunk * 256, chunk * 256 + 256)
+            part[DOWN, yy, lanes] = dot_tn(act[yy, :, lanes], g_all[...]).astype(bf16)
+
+    def du_chunk(yy, chunk):
+        lanes = slice(chunk * 256, chunk * 256 + 256)
+
+        def body(tile, carry):
+            rows = rows_at(tile, 256)
+            grad = dot_nt(g_all[rows], full[DOWN, yy, lanes]) * slope[yy, rows, lanes].astype(f32)
+            grad = grad.astype(bf16)
+            slope[yy, rows, lanes] = grad
+            return carry + column_sums(grad.astype(f32))
+
+        total = lax.fori_loop(0, 3, body, jnp.zeros((1, 256), f32))
+        for cc in (0, 1):
+            for side in (0, 1):
+                row = UP_BIAS_ROW + 2 * cc + side
+                small[row : row + 1, lanes] = jnp.where(
+                    jnp.logical_and(core == cc, yy == side), total, small[row : row + 1, lanes]
+                )
+
+    def mlp_term(rows):
+        return dot_nn(act[0, rows], full[DOWN, 0]) + dot_nn(act[1, rows], full[DOWN, 1])
+
+    def du_term(rows):
+        return dot_nn(slope[0, rows], full[UP, 0]) + dot_nn(slope[1, rows], full[UP, 1])
+
+    def up_grad(yy):
+        for chunk in range(3):
+            lanes = slice(chunk * 256, chunk * 256 + 256)
+            part[UP, yy, lanes] = dot_tn(slope[yy, :, lanes], n2_all[...]).astype(bf16)
+
+    def second_norm_back():
+        def body(block, carry):
+            rows = rows_at(block, ROW)
+            grad = swapped(2, rows)
+            xhat, scale = row_stats(hidden1[rows])
+            scaled = grad * gains[1:2, :]
+            back = (
+                scaled
+                - jnp.mean(scaled, axis=-1, keepdims=True)
+                - xhat * jnp.mean(scaled * xhat, axis=-1, keepdims=True)
+            ) * scale
+            given = cotangent[rows].astype(f32)
+            total = given + back
+            input_grad[rows] = total
+            dh_all[place(core, block)] = total.astype(bf16)
+            hand_over(dh_all, 3, block).start()
+            small[1:2, :] += column_sums(grad * xhat)
+            small[6:7, :] += column_sums(grad)
+            small[5:6, :] += column_sums(total)
+            small[7:8, :] += column_sums(given)
+            return carry
+
+        lax.fori_loop(0, 3, body, 0)
+
+    def project_back(yy):
+        def body(tile, carry):
+            rows = rows_at(tile, 256)
+            datt[yy, rows] = dot_nn(dh_all[rows], full[ATTN, yy, :, 512:768]).astype(bf16)
+            return carry
+
+        lax.fori_loop(0, 3, body, 0)
+
+    def attend_back(yy, head):
+        key_acc[...] = jnp.zeros_like(key_acc)
+        value_acc[...] = jnp.zeros_like(value_acc)
+
+        def body(tile, carry):
+            rows = rows_at(tile, 256)
+            keys = rows_at(tile // 2, PACK)
+            queries, key_rows, values = head_rows(yy, head, rows, keys)
+            grad = datt[yy, rows, HD + HD * head : 2 * HD + HD * head]
+            weights = probs[yy * 3 + head, tile]
+            weights_full = weights.astype(f32)
+            back = dot_nt(values, grad) * weights_full
+            center = jnp.sum(back, axis=0, keepdims=True)
+            grad_scores = (back - weights_full * center).astype(bf16)
+            grad_queries = dot_tn(key_rows, grad_scores) * HD ** (-0.5)
+            value_acc[keys] += dot_nn(weights, grad)
+            key_acc[keys] += dot_nn(grad_scores, queries)
+            qkv[yy, rows, 384 + HD * head : 448 + HD * head] = grad_queries.T.astype(bf16)
+            return carry
+
+        lax.fori_loop(0, 3, body, 0)
+        qkv[yy, :, HD * head : HD * head + HD] = key_acc[...].astype(bf16)
+        qkv[yy, :, 192 + HD * head : 256 + HD * head] = value_acc[...].astype(bf16)
+
+    def send_far(yy):
+        start(qkv.at[yy, far_rows, 0:384], dkv_far.at[yy], far_s.at[2 + yy], far_r.at[2 + yy], y_side)
+
+    def add_far(yy):
+        copy(
+            qkv.at[yy, far_rows, 0:384], dkv_far.at[yy], far_s.at[2 + yy], far_r.at[2 + yy], y_side
+        ).wait_recv()
+        qkv[yy, half_rows, 0:384] = (
+            qkv[yy, half_rows, 0:384].astype(f32) + dkv_far[yy].astype(f32)
+        ).astype(bf16)
+
+    def finish_act():
+        def body(block, carry):
+            rows = rows_at(block, ROW)
+            act_out[rows] = (hidden1[rows] + swapped(1, rows) + biases[5:6, :]).astype(bf16)
+            return carry
+
+        lax.fori_loop(0, 3, body, 0)
+
+    def attn_grad(yy):
+        for chunk in range(3):
+            lanes = slice(chunk * 256, chunk * 256 + 256)
+            n1_part = n1_all[0:CHIP, lanes]
+            part[ATTN, yy, lanes, 0:512] = dot_tn(n1_part, qkv[yy, 0:CHIP, 0:512]).astype(bf16)
+            part[ATTN, yy, lanes, 512:768] = (
+                dot_tn(n1_part, qkv[yy, 0:CHIP, 512:768]) + dot_tn(dh_all[:, lanes], att[yy])
+            ).astype(bf16)
+
+    def in_term(rows):
+        return dot_nt(qkv[0, rows], full[ATTN, 0]) + dot_nt(qkv[1, rows], full[ATTN, 1])
+
+    def head_bias_sums():
+        for yy in (0, 1):
+            sums = column_sums(qkv[yy, 0:CHIP, 192:576].astype(f32))
+            for cc in (0, 1):
+                first = yy * 384 + cc * 192
+                small[4:5, first : first + 192] = jnp.where(core == cc, sums[:, 0:192], 0.0)
+                small[3:4, first : first + 192] = jnp.where(core == cc, sums[:, 192:384], 0.0)
+
+    def first_norm_back():
+        def body(block, carry):
+            rows = rows_at(block, ROW)
+            grad = swapped(3, rows)
+            xhat, scale = row_stats(embedded[rows])
+            scaled = grad * gains[0:1, :]
+            back = (
+                scaled
+                - jnp.mean(scaled, axis=-1, keepdims=True)
+                - xhat * jnp.mean(scaled * xhat, axis=-1, keepdims=True)
+            ) * scale
+            total = input_grad[rows] + back
+            input_grad[rows] = total
+            small[0:1, :] += column_sums(grad * xhat)
+            small[2:3, :] += column_sums(grad)
+            image = type_cols[rows, 0:1] > 0
+            small[8:9, :] += column_sums(jnp.where(image, 0.0, total))
+            small[9:10, :] += column_sums(jnp.where(image, total, 0.0))
+            return carry
+
+        lax.fori_loop(0, 3, body, 0)
+
+    def small_core():
+        start(small, small_recv.at[4], small_s.at[4], small_r.at[4], sibling)
+
+    def small_x():
+        copy(small, small_recv.at[4], small_s.at[4], small_r.at[4], sibling).wait_recv()
+        small_recv[5] = small[...] + small_recv[4]
+        start(small_recv.at[5], small_recv.at[6], small_s.at[5], small_r.at[5], x_side)
+
+    def small_y():
+        copy(small_recv.at[5], small_recv.at[6], small_s.at[5], small_r.at[5], x_side).wait_recv()
+        small_recv[7] = small_recv[5] + small_recv[6]
+        start(small_recv.at[7], small_recv.at[8], small_s.at[6], small_r.at[6], y_side)
+
+    def small_z():
+        copy(small_recv.at[7], small_recv.at[8], small_s.at[6], small_r.at[6], y_side).wait_recv()
+        small_recv[z] = small_recv[7] + small_recv[8]
+        for j in (1, 2, 3):
+            start(small_recv.at[z], small_recv.at[z], small_s.at[j], small_r.at[j], z_side[j])
+
+    def small_done():
+        for j in (1, 2, 3):
+            there = small_recv.at[z_of[j]]
+            copy(there, there, small_s.at[j], small_r.at[j], z_side[j]).wait_recv()
+        small_out[...] = (small_recv[0] + small_recv[1]) + (small_recv[2] + small_recv[3])
+
+    def attn_out_rows():
+        qkv_grad[0] = attn_out[:, 384:576]
+        qkv_grad[1] = attn_out[:, 0:192]
+        qkv_grad[2] = attn_out[:, 192:384]
+        out_grad[...] = attn_out[:, 576:768].T
+
+    own_attn()
+    gather_on(ATTN, 0)
+    gather_z(ATTN)
+    own_rest()
+    column_types()
+    gather_on(UP, 0)
+    gather_on(ATTN, 1)
+    gather_far(UP, 0)
+    bias_along_z()
+    gather_on(ATTN, 2)
+    first_norm()
+    gather_z(UP)
+    half_over()
+    gather_last(UP)
+    spread_done(n1_all, 1)
+    gather_on(ATTN, 3)
+    bias_along_x()
+    masks()
+    gather_far(ATTN, 1)
+    gather_far(ATTN, 0)
+    gather_far(ATTN, 2)
+    half_relay()
+    gather_far(ATTN, 3)
+    zeros_and_biases()
+    gather_on(DOWN, 0)
+    half_arrived()
+    give_cotangent()
+    gather_on(UP, 1)
+    project(y)
+    gather_on(UP, 2)
+    gather_z(DOWN)
+    gather_done(ATTN)
+    project(1 - y)
+    gather_far(DOWN, 0)
+    bias_along_y()
+    attend(y, 0)
+    gather_relay(UP)
+    attend(y, 1)
+    attend(y, 2)
+    gather_on(DOWN, 2)
+    gather_last(DOWN)
+    gather_on(DOWN, 1)
+    attend(1 - y, 0)
+    attend(1 - y, 1)
+    gather_last_done(UP)
+    gather_on(UP, 3)
+    gather_far(UP, 2)
+    attend(1 - y, 2)
+    gather_on(DOWN, 3)
+    swap_sums(0, out_term)
+    gather_far(UP, 1)
+    gather_far(UP, 3)
+    spread_done(g_all, 0)
+    swap_done(0)
+    second_norm()
+    bias_as_rows()
+    gather_done(UP)
+    gather_far(DOWN, 2)
+    spread_done(n2_all, 2)
+    up_chunk(y, 0)
+    gather_far(DOWN, 1)
+    up_chunk(y, 1)
+    gather_far(DOWN, 3)
+    gather_relay(DOWN)
+    up_chunk(y, 2)
+    up_chunk(1 - y, 0)
+    up_chunk(1 - y, 1)
+    up_chunk(1 - y, 2)
+    gather_last_done(DOWN)
+    down_grad(1 - y)
+    down_grad(y)
+    scatter_last(DOWN)
+    du_chunk(y, 0)
+    du_chunk(y, 1)
+    scatter_far(DOWN, 3)
+    du_chunk(y, 2)
+    gather_done(DOWN)
+    du_chunk(1 - y, 0)
+    du_chunk(1 - y, 1)
+    scatter_far(DOWN, 2)
+    du_chunk(1 - y, 2)
+    swap_sums(2, du_term)
+    up_grad(y)
+    up_grad(1 - y)
+    scatter_far(UP, 3)
+    swap_done(2)
+    second_norm_back()
+    scatter_far(UP, 2)
+    scatter_far(UP, 1)
+    scatter_last(UP)
+    scatter_near(DOWN, 2)
+    scatter_near(DOWN, 3)
+    spread_done(dh_all, 3)
+    scatter_far(DOWN, 1)
+    project_back(0)
+    scatter_near(UP, 3)
+    project_back(1)
+    scatter_near(UP, 2)
+    scatter_relay(DOWN)
+    attend_back(0, 0)
+    scatter_near(UP, 1)
+    attend_back(0, 1)
+    attend_back(0, 2)
+    attend_back(1, 0)
+    send_far(0)
+    attend_back(1, 1)
+    attend_back(1, 2)
+    send_far(1)
+    swap_sums(1, mlp_term)
+    scatter_near(DOWN, 1)
+    scatter_z(DOWN, 3)
+    add_far(0)
+    swap_done(1)
+    scatter_z(UP, 3)
+    add_far(1)
+    attn_grad(1 - y)
+    scatter_far(ATTN, 0)
+    scatter_far(ATTN, 1)
+    scatter_far(ATTN, 2)
+    attn_grad(y)
+    finish_act()
+    scatter_far(ATTN, 3)
+    swap_sums(3, in_term)
+    scatter_z(DOWN, 2)
+    swap_done(3)
+    scatter_relay(UP)
+    scatter_near(ATTN, 1)
+    scatter_near(ATTN, 3)
+    scatter_last_add(DOWN)
+    scatter_z(UP, 2)
+    scatter_z(DOWN, 1)
+    scatter_z(ATTN, 1)
+    scatter_near(ATTN, 0)
+    head_bias_sums()
+    first_norm_back()
+    small_core()
+    scatter_far(DOWN, 0)
+    scatter_z(UP, 1)
+    scatter_z(ATTN, 3)
+    small_x()
+    scatter_near(ATTN, 2)
+    scatter_last_add(UP)
+    scatter_z(ATTN, 0)
+    small_y()
+    scatter_far(UP, 0)
+    scatter_near(DOWN, 0)
+    small_z()
+    scatter_z(ATTN, 2)
+    small_done()
+    scatter_near(UP, 0)
+    scatter_z(DOWN, 0)
+    scatter_done(ATTN)
+    attn_out_rows()
+    scatter_z(UP, 0)
+    scatter_done(DOWN)
+    scatter_done(UP)
+    for one in pending:
+        one.wait_send()
+    for which, one in pending_if:
+        @pl.when(which)
+        def _(one=one):
+            one.wait_send()
+
+    @pl.when(holds_half)
+    def _():
+        over_y.wait_send()
+
+    @pl.when(jnp.logical_not(holds_half))
+    def _():
+        relay.wait_send()
+
+
+def run_layer(*operands):
+    f32, bf16 = jnp.float32, jnp.bfloat16
+    vmem, dma = pltpu.VMEM, pltpu.SemaphoreType.DMA
+    scratch = [
+        vmem((3, 2, 768, 768), bf16),
+        vmem((3, 2, 768, 768), bf16),
+        vmem((CHIP, 768), bf16),
+        vmem((CHIP + HALF_PACK, 768), bf16),
+        vmem((CHIP, 768), bf16),
+        vmem((CHIP, 768), bf16),
+        vmem((2, CHIP + HALF_PACK, 768), bf16),
+        vmem((2, CHIP, 256), bf16),
+        vmem((2, HALF_PACK, 384), bf16),
+        vmem((6, 3, PACK, 256), bf16),
+        vmem((3, PACK, 256), bf16),
+        vmem((2, CHIP, 768), bf16),
+        vmem((2, CHIP, 768), bf16),
+        vmem((2, CHIP, 256), bf16),
+        vmem((CHIP + HALF_PACK, HD), f32),
+        vmem((CHIP + HALF_PACK, HD), f32),
+        vmem((OWN, 768), f32),
+        vmem((OWN, 768), f32),
+        vmem((OWN, 768), f32),
+        vmem((BLK, 768), f32),
+        vmem((OWN, 768), bf16),
+        vmem((4, OWN, 768), bf16),
+        vmem((OWN, 128), f32),
+        vmem((2, 1, 640), f32),
+        vmem((16, 8, 128), f32),
+        vmem((2, 8, 768), f32),
+        vmem((SMALL_ROWS, 768), f32),
+        vmem((9, SMALL_ROWS, 768), f32),
+        vmem((3, 4, BLK, 768), bf16),
+        vmem((3, 4, BLK, 768), bf16),
+        vmem((3, 4, 64, 768), bf16),
+        vmem((3, 4, 64, 768), bf16),
+        vmem((3, 4, BLK, 768), bf16),
+        vmem((2, 4, 2, 2 * Z_LAST, 768), bf16),
+    ]
+    scratch += [dma((3, 4))] * 24 + [dma((3, 8))] * 4
+    scratch += [dma((4, 3))] * 4 + [dma((4,))] * 2 + [dma((6,))] * 2 + [dma((7,))] * 2
+    whole = pl.BlockSpec(memory_space=vmem)
+    return pl.pallas_call(
+        layer_kernel,
+        out_shape=(
+            jax.ShapeDtypeStruct((OWN, 768), bf16),
+            jax.ShapeDtypeStruct((OWN, 768), f32),
+            jax.ShapeDtypeStruct((3, BLK, 192), f32),
+            jax.ShapeDtypeStruct((192, BLK), f32),
+            jax.ShapeDtypeStruct((BLK, 768), f32),
+            jax.ShapeDtypeStruct((BLK, 768), f32),
+            jax.ShapeDtypeStruct((SMALL_ROWS, 768), f32),
+        ),
+        in_specs=[whole] * len(operands),
+        out_specs=(whole,) * 7,
+        scratch_shapes=scratch,
+        compiler_params=pltpu.CompilerParams(
+            collective_id=0, has_side_effects=True, vmem_limit_bytes=63 * 2**20
+        ),
+    )(*operands)
+
+
+def fits_kernel(mesh):
+    return dict(mesh.shape) == {"wide": 8, "narrow": 4}
+
+
+def fused_shards(
+    tokens,
+    type_ids,
+    segment_ids,
+    cotangent,
+    type_table,
+    type_first,
+    type_second,
+    norm_gains,
+    gains_first,
+    gains_second,
+    biases,
+    biases_first,
+    biases_second,
+    qkv_weight,
+    qkv_first,
+    qkv_second,
+    out_weight,
+    out_first,
+    out_second,
+    up_weight,
+    up_first,
+    up_second,
+    up_bias,
+    up_bias_first,
+    up_bias_second,
+    down_weight,
+    down_first,
+    down_second,
+):
+    wide, narrow = lax.axis_index("wide"), lax.axis_index("narrow")
+    y, core = narrow // 2, narrow % 2
+    activations, input_grad, grad_qkv, grad_out, grad_up, grad_down, small = run_layer(
+        qkv_weight, out_weight, up_weight.T, down_weight, up_bias[None, :], tokens, type_ids[None, :],
+        cotangent, segment_ids, type_table, norm_gains, biases,
+    )
+    grad_up = grad_up.T
+    bias_part = lax.dynamic_slice_in_dim(small, UP_BIAS_ROW + 2 * core + y, 1)[0]
+    grad_up_bias = jnp.concatenate(
+        [
+            lax.dynamic_slice_in_dim(bias_part, wide * 64, 64),
+            lax.dynamic_slice_in_dim(bias_part, LAST_AT + wide * Z_LAST, Z_LAST),
+        ]
+    )
+    step_sizes = step_rates()
+    updates = [
+        adam_update(type_table, type_first, type_second, small[8:10], step_sizes[0]),
+        adam_update(norm_gains, gains_first, gains_second, small[0:2], step_sizes[1]),
+        adam_update(biases, biases_first, biases_second, small[2:8], step_sizes[2]),
+        adam_update(qkv_weight, qkv_first, qkv_second, grad_qkv, step_sizes[3]),
+        adam_update(out_weight, out_first, out_second, grad_out, step_sizes[4]),
+        adam_update(up_weight, up_first, up_second, grad_up, step_sizes[5]),
+        adam_update(up_bias, up_bias_first, up_bias_second, grad_up_bias, step_sizes[6]),
+        adam_update(down_weight, down_first, down_second, grad_down, step_sizes[7]),
+    ]
+    return (activations, input_grad) + tuple(value for update in updates for value in update)
+
+
 def solution(mesh):
     placed = (
         P(("wide", "narrow"), None),
@@ -348,7 +1402,7 @@
         P(("wide", "narrow"), None),
     )
     return jax.shard_map(
-        shards,
+        fused_shards if fits_kernel(mesh) else shards,
         mesh=mesh,
         in_specs=placed,
         out_specs=(

time: 683 us -> 165 us (0.24); the launches traced: 673 us -> 165 us
  waiting for transfers between devices: 297 us -> 0 us
  Pallas kernels: 0 us -> 150 us
  blocking collectives: 149 us -> 0 us
  matrix products: 90.7 us -> 0 us
  local copies, waits for them, and re-layouts: 64.8 us -> 4.83 us
  other arithmetic: 43.8 us -> 8.46 us
  between operations: 17.1 us -> 0.93 us
  starting transfers between devices: 11 us -> 0 us
    reduce_scatter x4 -> x0, waiting for transfers between devices: 179 us -> none  [the longest x1 139 us: shards(): lax.psum_scatter(grad_down, ('wide', 'narrow'), scatter_dimension=0, tile...]
    pallas_call x0 -> x1, Pallas kernels: none -> 150 us  [run_layer(): pl.pallas_call(layer_kernel, out_shape=(jax.ShapeDtypeStruct((OWN, 768),...]
    all_gather x4 -> x0, waiting for transfers between devices: 103 us -> none  [the longest x1 58.8 us: shards(): lax.all_gather(down_low, ('wide', 'narrow'), axis=0, tiled=True)]
    dot_general x32 -> x0, matrix products: 87.4 us -> none  [the longest x3 22.3 us: times_transposed(): lax.dot_general(left_mat, right_mat, (((1,), (1,)), ((), ())), preferred_...]
    all_gather x2 -> x0, blocking collectives: 70.1 us -> none  [the longest x1 39 us: shards(): lax.all_gather(qkv_low, 'wide', axis=1, tiled=True)]
    psum x1 -> x0, blocking collectives: 40.1 us -> none  [shards(): lax.psum((gain_part, shift_part, type_part), ('wide', 'narrow'))]
    unnamed x1 -> x0, blocking collectives: 39.1 us -> none
    reduce_sum x14 -> x0, other arithmetic: 18.2 us -> none  [the longest x2 3.65 us: norm_rows(): return spread * lax.rsqrt(variance + norm_eps) * gain + shift]
  transfers between devices with their start and end apart: 10 -> 0, of which waited for: 7 -> 0; matrix products, arithmetic and copies ran while one was open for 12% -> 0% of each run, Pallas kernels for 0% -> 0%
where the time goes in v2:
time: 165 us
  Pallas kernels  150 us (91%)
  other arithmetic  8.46 us (5%)
  local copies, waits for them, and re-layouts  4.83 us (3%)
    pallas_call x1, Pallas kernels, run_layer(): pl.pallas_call(layer_kernel, out_shape=(jax.ShapeDtypeStruct((OWN, 768),...  150 us
    sub x7, other arithmetic, adam_update(): weight_in - step_rate * (direction + 0.01 * weight_in)  8.46 us

profile of v2, /device:TPU:0, one launch (start us, length us, event | category | flops | bytes accessed | tf_op | source)
XLA Modules:
  0.0 164.6 jit_solution(12443553905206779587)
XLA Ops:
  0.7 0.0 copy-start.18
  0.7 0.0 copy-start.19
  0.7 0.0 copy-start.14
  0.7 0.0 copy-start.22
  0.7 0.0 copy-start.20
  0.7 0.0 copy-start.21
  0.7 1.3 broadcast_in_dim.7.type_ids
  2.0 150.4 %shard_map.467 = (bf16[384,768]{1,0:T(8,128)(2,1)}, f32[384,768]{1,0:T(8,128)}, f32[3,96,192]{2,1,0:T(8,128)}, f32[192,96]{1,0:T(8,128)}, f32[96,768]{1,0:T(8,12...) custom-call(f32[3,96,192]{2,1,0:T(8,128)} %qkv_weight.1, f32[192,96]{1,0:T(8,128)} %out_weight.1, f32[96,768]{1,0:T(8,128)} %bitcast.11, ...), custom_call_target="tpu_custom_call" | custom-call | tf_op jit(solution)/shard_map/pallas_call | solution.py:1291
  152.4 0.0 copy-start.5
  152.4 0.0 copy-start.15
  152.4 0.0 copy-start.16
  152.4 0.0 copy-start.17
  152.4 0.0 copy-done.18
  152.5 0.0 copy-done.19
  152.5 0.0 copy-done.22
  152.5 1.5 multiply_subtract_fusion.5
  154.0 0.0 copy-done.14
  154.0 0.0 copy-done.20
  154.0 0.0 copy-done.21
  154.0 1.4 multiply_subtract_fusion.4
  155.4 0.0 copy-done
  155.4 0.0 copy-done.6
  155.4 0.0 copy-start.1
  155.4 0.0 copy-start.8
  155.4 0.0 copy-start.9
  155.5 2.1 %multiply_subtract_fusion.2 = (f32[3,96,192]{2,1,0:T(8,128)}, f32[3,96,192]{2,1,0:T(8,128)}, f32[3,96,192]{2,1,0:T(8,128)}) fusion(f32[3,96,192]{2,1,0:T(8,128)S(1)} %copy-done, f32[3,96,192]{2,1,0:T(8,128)} %get-tuple-element.36, f32[3,96,192]{2,1,0:T(8,128)S(1)} %copy-done.6, f32[3,96,192]{2,1,0:T(8,128)S(1)} %copy-done.7), kind=kLoop, calls=%fused_computation.11 | loop fusion | flops 774144 | bytes 1548288 | tf_op jit(solution)/shard_map/sub | solution.py:60
  157.6 0.0 copy-done.5
  157.6 0.0 copy-done.16
  157.6 0.7 multiply_subtract_fusion.3
  158.3 0.0 copy-start.10
  158.3 0.0 copy-start.11
  158.4 0.0 copy-start.12
  158.4 0.0 copy-done.1
  158.4 0.0 copy-done.8
  158.4 0.0 copy-done.9
  158.4 0.0 copy-done.13
  158.4 1.1 multiply_subtract_fusion.1
  159.5 0.8 dynamic-slice_bitcast_fusion
  160.3 0.8 dynamic-slice_bitcast_fusion.1
  161.1 0.0 copy-done.24
  161.1 0.6 multiply_subtract_fusion.7
  161.7 0.0 copy-done.11
  161.7 0.0 copy-done.12
  161.7 0.0 copy-start.3
  161.7 1.1 multiply_subtract_fusion
  162.8 0.0 copy-done.4
  162.8 0.8 copy.56
  163.6 1.0 copy.57
  (17 shorter events, 0.0 us)
Async XLA Ops:
  0.7 151.8 %copy-start.18 = (f32[2,768]{1,0:T(2,128)S(1)}, f32[2,768]{1,0:T(2,128)}, u32[]{:S(2)}) copy-start(f32[2,768]{1,0:T(2,128)} %type_table.1) | copy-start | bytes 18436
  0.7 151.8 %copy-start.19 = (f32[2,768]{1,0:T(2,128)S(1)}, f32[2,768]{1,0:T(2,128)}, u32[]{:S(2)}) copy-start(f32[2,768]{1,0:T(2,128)} %gains.1) | copy-start | bytes 18436
  0.7 153.3 %copy-start.14 = (f32[6,768]{1,0:T(8,128)S(1)}, f32[6,768]{1,0:T(8,128)}, u32[]{:S(2)}) copy-start(f32[6,768]{1,0:T(8,128)} %biases.1) | copy-start | bytes 55300
  0.7 151.8 %copy-start.22 = (f32[2,768]{1,0:T(2,128)S(1)}, f32[2,768]{1,0:T(2,128)}, u32[]{:S(2)}) copy-start(f32[2,768]{1,0:T(2,128)} %param.36) | copy-start | bytes 18436
  0.7 153.3 %copy-start.20 = (f32[6,768]{1,0:T(8,128)S(1)}, f32[6,768]{1,0:T(8,128)}, u32[]{:S(2)}) copy-start(f32[6,768]{1,0:T(8,128)} %param.39) | copy-start | bytes 55300
  0.7 153.3 %copy-start.21 = (f32[6,768]{1,0:T(8,128)S(1)}, f32[6,768]{1,0:T(8,128)}, u32[]{:S(2)}) copy-start(f32[6,768]{1,0:T(8,128)} %param.40) | copy-start | bytes 55300
  2.0 153.4 %copy-start = (f32[3,96,192]{2,1,0:T(8,128)S(1)}, f32[3,96,192]{2,1,0:T(8,128)}, u32[]{:S(2)}) copy-start(f32[3,96,192]{2,1,0:T(8,128)} %qkv_weight.1) | copy-start | bytes 663556
  2.0 153.4 %copy-start.6 = (f32[3,96,192]{2,1,0:T(8,128)S(1)}, f32[3,96,192]{2,1,0:T(8,128)}, u32[]{:S(2)}) copy-start(f32[3,96,192]{2,1,0:T(8,128)} %param.42) | copy-start | bytes 663556
  2.0 153.4 %copy-start.7 = (f32[3,96,192]{2,1,0:T(8,128)S(1)}, f32[3,96,192]{2,1,0:T(8,128)}, u32[]{:S(2)}) copy-start(f32[3,96,192]{2,1,0:T(8,128)} %param.43) | copy-start | bytes 663556
  152.4 5.2 %copy-start.5 = (f32[192,96]{1,0:T(8,128)S(1)}, f32[192,96]{1,0:T(8,128)}, u32[]{:S(2)}) copy-start(f32[192,96]{1,0:T(8,128)} %out_weight.1) | copy-start | bytes 221188
  152.4 5.2 %copy-start.15 = (f32[192,96]{1,0:T(8,128)S(1)}, f32[192,96]{1,0:T(8,128)}, u32[]{:S(2)}) copy-start(f32[192,96]{1,0:T(8,128)} %param.45) | copy-start | bytes 221188
  152.4 5.1 %copy-start.16 = (f32[192,96]{1,0:T(8,128)S(1)}, f32[192,96]{1,0:T(8,128)}, u32[]{:S(2)}) copy-start(f32[192,96]{1,0:T(8,128)} %param.46) | copy-start | bytes 221188
  152.4 5.1 %copy-start.17 = (f32[192,96]{1,0:T(8,128)S(1)}, f32[192,96]{1,0:T(8,128)}, u32[]{:S(2)}) copy-start(f32[192,96]{1,0:T(8,128)} %get-tuple-element.37) | copy-start | bytes 221188
  155.4 3.0 %copy-start.1 = (f32[768,96]{0,1:T(8,128)S(1)}, f32[768,96]{0,1:T(8,128)}, u32[]{:S(2)}) copy-start(f32[768,96]{0,1:T(8,128)} %param.47) | copy-start | bytes 884740
  155.4 3.0 %copy-start.8 = (f32[768,96]{0,1:T(8,128)S(1)}, f32[768,96]{0,1:T(8,128)}, u32[]{:S(2)}) copy-start(f32[768,96]{0,1:T(8,128)} %param.48) | copy-start | bytes 884740
  155.4 3.0 %copy-start.9 = (f32[768,96]{0,1:T(8,128)S(1)}, f32[768,96]{0,1:T(8,128)}, u32[]{:S(2)}) copy-start(f32[768,96]{0,1:T(8,128)} %param.49) | copy-start | bytes 884740
  155.4 3.0 %copy-start.13 = (f32[96,768]{1,0:T(8,128)S(1)}, f32[96,768]{1,0:T(8,128)}, u32[]{:S(2)}) copy-start(f32[96,768]{1,0:T(8,128)} %get-tuple-element.38) | copy-start | bytes 884740
  158.3 2.7 %copy-start.23 = (f32[96]{0:T(128)S(1)}, f32[96]{0:T(128)}, u32[]{:S(2)}) copy-start(f32[96]{0:T(128)} %param.50) | copy-start | bytes 1156
  158.3 2.7 %copy-start.24 = (f32[96]{0:T(128)S(1)}, f32[96]{0:T(128)}, u32[]{:S(2)}) copy-start(f32[96]{0:T(128)} %param.51) | copy-start | bytes 1156
  158.3 2.7 %copy-start.25 = (f32[96]{0:T(128)S(1)}, f32[96]{0:T(128)}, u32[]{:S(2)}) copy-start(f32[96]{0:T(128)} %param.52) | copy-start | bytes 1156
  158.3 3.4 %copy-start.2 = (f32[96,768]{1,0:T(8,128)S(1)}, f32[96,768]{1,0:T(8,128)}, u32[]{:S(2)}) copy-start(f32[96,768]{1,0:T(8,128)} %down_rows.1) | copy-start | bytes 884740
  158.3 3.4 %copy-start.10 = (f32[96,768]{1,0:T(8,128)S(1)}, f32[96,768]{1,0:T(8,128)}, u32[]{:S(2)}) copy-start(f32[96,768]{1,0:T(8,128)} %param.54) | copy-start | bytes 884740
  158.3 3.3 %copy-start.11 = (f32[96,768]{1,0:T(8,128)S(1)}, f32[96,768]{1,0:T(8,128)}, u32[]{:S(2)}) copy-start(f32[96,768]{1,0:T(8,128)} %param.55) | copy-start | bytes 884740
  158.4 3.3 %copy-start.12 = (f32[96,768]{1,0:T(8,128)S(1)}, f32[96,768]{1,0:T(8,128)}, u32[]{:S(2)}) copy-start(f32[96,768]{1,0:T(8,128)} %get-tuple-element.39) | copy-start | bytes 884740
  159.5 3.3 %copy-start.4 = (bf16[384,768]{1,0:T(8,128)(2,1)S(1)}, bf16[384,768]{1,0:T(8,128)(2,1)}, u32[]{:S(2)}) copy-start(bf16[384,768]{1,0:T(8,128)(2,1)} %get-tuple-element.93) | copy-start | bytes 1769476
  161.7 1.9 %copy-start.3 = (f32[384,768]{1,0:T(8,128)S(1)}, f32[384,768]{1,0:T(8,128)}, u32[]{:S(2)}) copy-start(f32[384,768]{1,0:T(8,128)} %get-tuple-element.94) | copy-start | bytes 3538948
